TPU v7x, 32 devices: a whole 2x2x4 slice. The times are simulated.
32 devices in a mesh: depth: 4 (over y, x), scan: 8 (over z, core).
Axes of the slice: x: 2, y: 2, z: 4, core: 2. Of those that a mesh axis runs over, the one named last changes fastest.
Arguments:
- object_slice: bfloat16 [2, 4, 512, 2048], P(None, None, 'depth', 'scan'), may hold values from -4 to 4
- probe_field: bfloat16 [2, 512, 512], replicated, may hold values from -2 to 2
- offsets: int32 [16, 2], replicated, may hold values from 0 to 1536
- assignment: int32 [16], P('scan'), may hold values from 0 to 15, each once
- intensities: float32 [16, 512, 512], P('scan', 'depth'), may hold values from 0 to 3
Outputs:
- object_grad: float32 [2, 4, 512, 2048], P(None, None, 'depth', 'scan')
- probe_grad: float32 [2, 512, 512], P(None, 'depth')
Inputs may be any that keep to these rules, and one draw needn't show every extreme that they name: `offsets`: each window lies inside the object window. `assignment`: every position stands in exactly one slot; slots s * 2 to s * 2 + 1 lie on index s of scan.
All inputs are finite; a program needn't handle non-finite values.
Results may differ from a plain program's by a relative error of at most 0.0003.
Values may be sent and summed in bfloat16 or wider, within the bound.
A program may use at most 64 MiB of HBM per device.

v0:
```python
import math

import jax
import jax.numpy as jnp
from jax import lax
from jax.sharding import PartitionSpec as P

fresnel_scale = 4


def dft_table(size):
    index = jnp.arange(size, dtype=jnp.int32)
    turns = index[:, None] * index[None, :] % size
    angle = 2.0 * math.pi / size * turns.astype(jnp.float32)
    norm = 1.0 / math.sqrt(size)
    return (jnp.cos(angle) * norm, -jnp.sin(angle) * norm)


def chirp_phase(index, size):
    centred = index - size // 2
    period = 2 * fresnel_scale * size
    phase = centred * centred % period
    angle = math.pi / (fresnel_scale * size) * phase.astype(jnp.float32)
    return (jnp.cos(angle), jnp.sin(angle))


def contract(form, left_side, right_side):
    return jnp.einsum(
        form,
        left_side,
        right_side,
        precision=lax.Precision.HIGHEST,
        preferred_element_type=jnp.float32,
    )


def complex_mix(form, left_re, left_im, right_re, right_im):
    real_part = contract(form, left_re, right_re) - contract(form, left_im, right_im)
    imag_part = contract(form, left_re, right_im) + contract(form, left_im, right_re)
    return (real_part, imag_part)


def on_device(object_slice, probe_field, offsets, assignment, intensities):
    depth_index = lax.axis_index("depth")
    rows_dev = object_slice.shape[2]
    cycles = object_slice.shape[1]
    patch_side = probe_field.shape[2]
    pos_count = assignment.shape[0]
    total_pos = pos_count * lax.axis_size("scan")
    band_rows = lax.all_gather(object_slice, "scan", axis=3, tiled=True)
    full_width = band_rows.shape[3]
    flat_band = band_rows.reshape(2, cycles * rows_dev, full_width)
    position = offsets[assignment]
    top_row = position[:, 0]
    left_col = position[:, 1]
    table_re, table_im = dft_table(patch_side)
    row_ids = jnp.arange(rows_dev, dtype=jnp.int32)
    col_ids = jnp.arange(patch_side, dtype=jnp.int32)
    col_cos, col_sin = chirp_phase(col_ids, patch_side)
    zero_start = jnp.int32(0)

    def cut_tile(cycle_row, column):
        return lax.dynamic_slice(
            flat_band, (zero_start, cycle_row * rows_dev, column), (2, rows_dev, patch_side)
        )

    own_rows = depth_index * rows_dev + row_ids
    start_row = (depth_index * rows_dev - top_row) % patch_side
    patch_rows = (start_row[:, None] + row_ids[None, :]) % patch_side
    first_cycle = top_row // patch_side
    second_cycle = jnp.minimum(first_cycle + 1, cycles - 1)
    take_first = own_rows[None, :] >= (top_row % patch_side)[:, None]
    tiles_first = jax.vmap(cut_tile)(first_cycle, left_col)
    tiles_second = jax.vmap(cut_tile)(second_cycle, left_col)
    patch = jnp.where(take_first[:, None, :, None], tiles_first, tiles_second)
    doubled_probe = jnp.concatenate([probe_field, probe_field], 1)

    def probe_pick(first_row):
        return lax.dynamic_slice_in_dim(doubled_probe, first_row, rows_dev, 1)

    probe_rows = jax.vmap(probe_pick)(start_row)
    row_cos, row_sin = chirp_phase(patch_rows, patch_side)
    chirp_re = (
        row_cos[:, :, None] * col_cos[None, None, :] - row_sin[:, :, None] * col_sin[None, None, :]
    )
    chirp_im = (
        row_sin[:, :, None] * col_cos[None, None, :] + row_cos[:, :, None] * col_sin[None, None, :]
    )
    obj_re = patch[:, 0].astype(jnp.float32)
    obj_im = patch[:, 1].astype(jnp.float32)
    probe_re = probe_rows[:, 0].astype(jnp.float32)
    probe_im = probe_rows[:, 1].astype(jnp.float32)
    wave_re = probe_re * obj_re - probe_im * obj_im
    wave_im = probe_re * obj_im + probe_im * obj_re
    psi_re = wave_re * chirp_re - wave_im * chirp_im
    psi_im = wave_re * chirp_im + wave_im * chirp_re
    half_re, half_im = complex_mix("vk,pjk->pvj", table_re, table_im, psi_re, psi_im)
    half_re, half_im = (
        lax.all_to_all(half_re, "depth", split_axis=1, concat_axis=2, tiled=True),
        lax.all_to_all(half_im, "depth", split_axis=1, concat_axis=2, tiled=True),
    )
    far_re, far_im = complex_mix("pvj,ju->pvu", half_re, half_im, table_re, table_im)
    excess = far_re * far_re + far_im * far_im - intensities
    resid_re = excess * far_re
    resid_im = excess * far_im
    mid_re, mid_im = complex_mix("pvu,uj->pvj", resid_re, resid_im, table_re, -table_im)
    mid_re, mid_im = (
        lax.all_to_all(mid_re, "depth", split_axis=2, concat_axis=1, tiled=True),
        lax.all_to_all(mid_im, "depth", split_axis=2, concat_axis=1, tiled=True),
    )
    back_re, back_im = complex_mix("vk,pvj->pjk", table_re, -table_im, mid_re, mid_im)
    grad_re = back_re * chirp_re + back_im * chirp_im
    grad_im = back_im * chirp_re - back_re * chirp_im
    contrib = jnp.stack(
        [probe_re * grad_re + probe_im * grad_im, probe_re * grad_im - probe_im * grad_re], 1
    )
    term_re = obj_re * grad_re + obj_im * grad_im
    term_im = obj_re * grad_im - obj_im * grad_re
    grad_band = jnp.zeros((2, cycles * rows_dev, full_width), jnp.float32)

    def add_tile(band_now, tile_value, cycle_row, column):
        corner = (zero_start, cycle_row * rows_dev, column)
        current = lax.dynamic_slice(band_now, corner, (2, rows_dev, patch_side))
        return lax.dynamic_update_slice(band_now, current + tile_value, corner)

    probe_double = jnp.zeros((2, 2 * patch_side, patch_side), jnp.float32)
    for slot_index in range(pos_count):
        value = contrib[slot_index]
        mask_here = take_first[slot_index][None, :, None]
        grad_band = add_tile(
            grad_band,
            jnp.where(mask_here, value, 0.0),
            first_cycle[slot_index],
            left_col[slot_index],
        )
        grad_band = add_tile(
            grad_band,
            jnp.where(mask_here, 0.0, value),
            second_cycle[slot_index],
            left_col[slot_index],
        )
        term_here = jnp.stack([term_re[slot_index], term_im[slot_index]])
        current_rows = lax.dynamic_slice_in_dim(probe_double, start_row[slot_index], rows_dev, 1)
        probe_double = lax.dynamic_update_slice_in_dim(
            probe_double, current_rows + term_here, start_row[slot_index], 1
        )
    probe_full = probe_double[:, :patch_side] + probe_double[:, patch_side:]
    probe_part = lax.psum_scatter(probe_full, "depth", scatter_dimension=1, tiled=True)
    probe_grad = lax.psum(probe_part, "scan")
    object_grad = lax.psum_scatter(
        grad_band.reshape(2, cycles, rows_dev, full_width), "scan", scatter_dimension=3, tiled=True
    )
    return (object_grad, probe_grad * total_pos ** (-0.5))


def solution(mesh):
    return jax.shard_map(
        on_device,
        mesh=mesh,
        in_specs=(P(None, None, "depth", "scan"), P(), P(), P("scan"), P("scan", "depth", None)),
        out_specs=(P(None, None, "depth", "scan"), P(None, "depth", None)),
        check_vma=False,
    )
```

profile of v0, /device:TPU:0, one launch (start us, length us, event | category | flops | bytes accessed | tf_op | source)
XLA Modules:
  0.0 396.6 jit_solution(5509645274461775509)
XLA Ops:
  17.9 42.2 %all-gather.2.cloned.1.call-done = bf16[2,4,128,2048]{3,2,1,0:T(8,128)(2,1)} async-done(((bf16[2,4,128,256]{3,2,1,0:T(8,128)(2,1)}), bf16[2,4,128,2048]{3,2,1,0:T(8,128)(2,1)}) %all-gather.2.cloned.1.call-update) | async-done | bytes 4194320 | tf_op jit(solution)/shard_map/all_gather | solution.py:50
  60.2 6.7 %while.2 = (s32[]{:T(128)}, bf16[2,512,2048]{2,1,0:T(8,128)(2,1)}, s32[2,3]{1,0:T(2,128)S(1)}, bf16[2,2,128,512]{3,2,0,1:T(8,128)(2,1)S(1)}, s32[]{:T(128)}) while((s32[]{:T(128)}, bf16[2,512,2048]{2,1,0:T(8,128)(2,1)}, s32[2,3]{1,0:T(2,128)S(1)}, bf16[2,2,128,512]{3,2,0,1:T(8,128)(2,1)S(1)}, s32[]{:T(128)}) %tuple.78), condition=%wide.while_cond, body=%wide.while_body.sunk | while | flops 2 | bytes 524413 | solution.py:63
  66.9 6.2 %while.3 = (s32[]{:T(128)}, bf16[2,512,2048]{2,1,0:T(8,128)(2,1)}, s32[2,3]{1,0:T(2,128)S(1)}, bf16[2,2,128,512]{3,2,0,1:T(8,128)(2,1)S(1)}, s32[]{:T(128)}) while((s32[]{:T(128)}, bf16[2,512,2048]{2,1,0:T(8,128)(2,1)}, s32[2,3]{1,0:T(2,128)S(1)}, bf16[2,2,128,512]{3,2,0,1:T(8,128)(2,1)S(1)}, s32[]{:T(128)}) %tuple.79), condition=%wide.while_cond.1, body=%wide.while_body.1.sunk | while | flops 2 | bytes 524413 | solution.py:63
  73.2 5.3 %fusion.27 = f32[2,128,512]{2,1,0:T(8,128)S(1)} fusion(f32[512]{0:T(512)S(1)} %get-tuple-element.78, f32[2,128]{1,0:T(2,128)S(1)} %get-tuple-element.76, f32[512]{0:T(512)S(1)} %get-tuple-element.79, f32[2,128]{1,0:T(2,128)S(1)} %get-tuple-element.75, bf16[2,2,128,512]{3,2,0,1:T(8,128)(2,1)S(1)} %broadcast_select_fusion, ...), kind=kOutput, calls=%fused_computation.48 | convolution fusion | flops 811728896 | bytes 1579008 | tf_op jit(solution)/shard_map/vk,pjk->pvj/dot_general | solution.py:28
  78.5 5.3 %fusion.1 = f32[2,512,128]{1,2,0:T(8,128)S(1)} fusion(f32[2,128,512]{2,1,0:T(8,128)S(1)} %fusion.27, f32[512]{0:T(512)S(1)} %get-tuple-element.78, f32[2,128]{1,0:T(2,128)S(1)} %get-tuple-element.76, f32[512]{0:T(512)S(1)} %get-tuple-element.79, f32[2,128]{1,0:T(2,128)S(1)} %get-tuple-element.75, bf16[2,2,128,512]{3,2,0,1:T(8,128)(2,1)S(1)} %broadcast_select_fusion, ...), kind=kOutput, calls=%fused_computation.20 | convolution fusion | flops 812122112 | bytes 2103296 | tf_op jit(solution)/shard_map/vk,pjk->pvj/dot_general | solution.py:28
  84.8 3.9 all-to-all-start
  88.7 5.3 %fusion.23 = f32[2,128,512]{2,1,0:T(8,128)S(1)} fusion(f32[512]{0:T(512)S(1)} %get-tuple-element.78, f32[2,128]{1,0:T(2,128)S(1)} %get-tuple-element.76, f32[512]{0:T(512)S(1)} %get-tuple-element.79, f32[2,128]{1,0:T(2,128)S(1)} %get-tuple-element.75, bf16[2,2,128,512]{3,2,0,1:T(8,128)(2,1)S(1)} %broadcast_select_fusion, ...), kind=kOutput, calls=%fused_computation.44 | convolution fusion | flops 811728896 | bytes 1579008 | tf_op jit(solution)/shard_map/vk,pjk->pvj/dot_general | solution.py:28
  94.0 5.3 %fusion = f32[2,512,128]{1,2,0:T(8,128)S(1)} fusion(f32[2,128,512]{2,1,0:T(8,128)S(1)} %fusion.23, f32[512]{0:T(512)S(1)} %get-tuple-element.78, f32[2,128]{1,0:T(2,128)S(1)} %get-tuple-element.76, f32[512]{0:T(512)S(1)} %get-tuple-element.79, f32[2,128]{1,0:T(2,128)S(1)} %get-tuple-element.75, bf16[2,2,128,512]{3,2,0,1:T(8,128)(2,1)S(1)} %broadcast_select_fusion, ...), kind=kOutput, calls=%fused_computation.18 | convolution fusion | flops 812122112 | bytes 2103296 | tf_op jit(solution)/shard_map/vk,pjk->pvj/dot_general | solution.py:28
  100.3 4.4 %all-to-all-start.1 = ((f32[2,512,128]{2,0,1:T(2,128)}), f32[2,512,128]{2,0,1:T(2,128)S(1)}, u32[]{:S(2)}, u32[]{:S(2)}) async-start(f32[2,512,128]{2,0,1:T(2,128)} %copy.40), calls=%async_computation.1 | async-start | bytes 1048576 | tf_op jit(solution)/shard_map/all_to_all | solution.py:100
  105.2 5.8 %fusion.25 = f32[2,128,512]{2,1,0:T(8,128)} fusion(f32[2,128,512]{2,1,0:T(8,128)S(1)} %all_to_all.55), kind=kOutput, calls=%fused_computation.46 | convolution fusion | flops 809238528 | bytes 1048576 | tf_op jit(solution)/shard_map/pvj,ju->pvu/dot_general | solution.py:28
  111.0 5.8 %fusion.10 = f32[2,128,512]{2,1,0:T(8,128)} fusion(f32[2,128,512]{2,1,0:T(8,128)S(1)} %all_to_all.55), kind=kOutput, calls=%fused_computation.31 | convolution fusion | flops 809500672 | bytes 1048576 | tf_op jit(solution)/shard_map/pvj,ju->pvu/dot_general | solution.py:28
  117.4 6.3 %convolution_add_fusion.2 = f32[2,128,512]{2,1,0:T(8,128)S(1)} fusion(f32[2,128,512]{2,1,0:T(8,128)} %fusion.10, f32[2,128,512]{2,1,0:T(8,128)S(1)} %all_to_all.59), kind=kOutput, calls=%fused_computation.15 | convolution fusion | flops 809369600 | bytes 1572864 | tf_op jit(solution)/shard_map/pvj,ju->pvu/dot_general | solution.py:28
  123.8 6.9 %convolution_subtract_fusion.2 = f32[2,128,512]{2,1,0:T(8,128)S(1)} fusion(f32[2,128,512]{2,1,0:T(8,128)} %fusion.25, f32[2,128,512]{2,1,0:T(8,128)S(1)} %all_to_all.59), kind=kOutput, calls=%fused_computation.16 | convolution fusion | flops 809631744 | bytes 1572864 | tf_op jit(solution)/shard_map/pvj,ju->pvu/dot_general | solution.py:28
  130.7 5.0 %fusion.7 = f32[2,128,512]{2,1,0:T(8,128)S(1)} fusion(f32[2,128,512]{2,1,0:T(8,128)S(1)} %convolution_subtract_fusion.2, f32[2,128,512]{2,1,0:T(8,128)S(1)} %copy-done.2, f32[2,128,512]{2,1,0:T(8,128)S(1)} %convolution_add_fusion.2), kind=kOutput, calls=%fused_computation.28 | convolution fusion | flops 810418176 | bytes 2097152 | tf_op jit(solution)/shard_map/pvu,uj->pvj/dot_general | solution.py:28
  135.7 5.0 %convolution_add_fusion.1 = f32[2,128,512]{2,1,0:T(8,128)S(1)} fusion(f32[2,128,512]{2,1,0:T(8,128)S(1)} %fusion.7, f32[2,128,512]{2,1,0:T(8,128)S(1)} %convolution_add_fusion.2, f32[2,128,512]{2,1,0:T(8,128)S(1)} %copy-done.2, f32[2,128,512]{2,1,0:T(8,128)S(1)} %convolution_subtract_fusion.2), kind=kOutput, calls=%fused_computation.13 | convolution fusion | flops 810024960 | bytes 2621440 | tf_op jit(solution)/shard_map/pvu,uj->pvj/dot_general | solution.py:28
  141.7 4.4 %all-to-all-start.3 = ((f32[2,128,512]{1,0,2:T(2,128)}), f32[2,128,512]{1,0,2:T(2,128)S(1)}, u32[]{:S(2)}, u32[]{:S(2)}) async-start(f32[2,128,512]{1,0,2:T(2,128)} %copy.44), calls=%async_computation.3 | async-start | bytes 1048576 | tf_op jit(solution)/shard_map/all_to_all | solution.py:109
  146.1 6.3 %fusion.20 = f32[2,128,512]{2,1,0:T(8,128)S(1)} fusion(f32[2,128,512]{2,1,0:T(8,128)} %copy-done.5, f32[2,128,512]{2,1,0:T(8,128)S(1)} %copy-done.2, f32[2,128,512]{2,1,0:T(8,128)} %copy-done.3), kind=kOutput, calls=%fused_computation.41 | convolution fusion | flops 809893888 | bytes 2097152 | tf_op jit(solution)/shard_map/pvu,uj->pvj/dot_general | solution.py:28
  152.4 5.0 %convolution_subtract_fusion.1 = f32[2,128,512]{2,1,0:T(8,128)S(1)} fusion(f32[2,128,512]{2,1,0:T(8,128)S(1)} %fusion.20, f32[2,128,512]{2,1,0:T(8,128)S(1)} %copy-done.4, f32[2,128,512]{2,1,0:T(8,128)S(1)} %copy-done.2, f32[2,128,512]{2,1,0:T(8,128)S(1)} %copy-done.6), kind=kOutput, calls=%fused_computation.14 | convolution fusion | flops 810549248 | bytes 2621440 | tf_op jit(solution)/shard_map/pvu,uj->pvj/dot_general | solution.py:28
  158.5 4.2 %all-to-all-start.2 = ((f32[2,128,512]{1,0,2:T(2,128)}), f32[2,128,512]{1,0,2:T(2,128)S(1)}, u32[]{:S(2)}, u32[]{:S(2)}) async-start(f32[2,128,512]{1,0,2:T(2,128)} %copy.42), calls=%async_computation.2 | async-start | bytes 1048576 | tf_op jit(solution)/shard_map/all_to_all | solution.py:108
  167.6 6.0 %fusion.15 = f32[2,128,512]{2,1,0:T(8,128)} fusion(f32[2,512,128]{1,2,0:T(8,128)S(1)} %all_to_all.67), kind=kOutput, calls=%fused_computation.36 | convolution fusion | flops 809238528 | bytes 1048576 | tf_op jit(solution)/shard_map/vk,pvj->pjk/dot_general | solution.py:28
  174.2 5.3 %fusion.18 = f32[2,128,512]{2,1,0:T(8,128)S(1)} fusion(f32[2,512,128]{1,2,0:T(8,128)S(1)} %all_to_all.63), kind=kOutput, calls=%fused_computation.39 | convolution fusion | flops 809238528 | bytes 1048576 | tf_op jit(solution)/shard_map/vk,pvj->pjk/dot_general | solution.py:28
  179.5 5.6 %convolution_subtract_fusion = f32[2,128,512]{2,1,0:T(8,128)S(1)} fusion(f32[2,128,512]{2,1,0:T(8,128)S(1)} %fusion.18, f32[2,512,128]{1,2,0:T(8,128)S(1)} %copy-done.1), kind=kOutput, calls=%fused_computation.12 | convolution fusion | flops 809893888 | bytes 1572864 | tf_op jit(solution)/shard_map/vk,pvj->pjk/dot_general | solution.py:28
  185.2 5.2 %fusion.41 = (f32[2,128,512]{2,1,0:T(8,128)S(1)}, f32[2,128,512]{2,1,0:T(8,128)S(1)}, f32[2,128,512]{2,1,0:T(8,128)S(1)}) fusion(bf16[2,2,128,512]{3,2,0,1:T(8,128)(2,1)S(1)} %broadcast_select_fusion, f32[2,128,512]{2,1,0:T(8,128)S(1)} %convolution_subtract_fusion, f32[512]{0:T(512)S(1)} %get-tuple-element.78, f32[2,128]{1,0:T(2,128)S(1)} %get-tuple-element.76, ...), kind=kOutput, calls=%fused_computation.76 | convolution fusion | flops 812122112 | bytes 3676160 | tf_op jit(solution)/shard_map/vk,pvj->pjk/dot_general | solution.py:28
  201.5 4.1 %slice_add_fusion = f32[2,512,512]{2,1,0:T(8,128)} fusion(f32[2,1024,512]{2,1,0:T(8,128)} %dynamic_update_slice.23), kind=kLoop, calls=%fused_computation.6 | loop fusion | flops 524288 | bytes 6291456 | tf_op jit(solution)/shard_map/add | solution.py:147
  213.5 4.3 %broadcast_in_dim.71 = f32[2,512,2048]{2,1,0:T(8,128)} broadcast(f32[]{:T(128)} %constant.95.clone.1), dimensions={} | broadcast | bytes 8388612 | tf_op jit(solution)/shard_map/broadcast_in_dim | solution.py:119
  217.9 4.7 %dynamic_update_slice.18 = f32[2,512,2048]{2,1,0:T(8,128)} dynamic-update-slice(f32[2,512,2048]{2,1,0:T(8,128)} %broadcast_in_dim.71, f32[2,128,512]{2,1,0:T(8,128)S(1)} %broadcast_select_fusion.1, s32[]{:T(128)} %constant.98.clone.1, s32[]{:T(128)S(6)} %select_n.193, s32[]{:T(128)S(6)} %select_n.194) | dynamic-update-slice | bytes 1048580 | tf_op jit(solution)/shard_map/dynamic_update_slice | solution.py:124
  224.0 4.8 %dynamic_update_slice.19 = f32[2,512,2048]{2,1,0:T(8,128)} dynamic-update-slice(f32[2,512,2048]{2,1,0:T(8,128)} %dynamic_update_slice.18, f32[2,128,512]{2,1,0:T(8,128)S(1)} %select_add_fusion.2, s32[]{:T(128)} %constant.98.clone.1, s32[]{:T(128)S(6)} %select_n.195, s32[]{:T(128)S(6)} %select_n.194) | dynamic-update-slice | bytes 1048580 | tf_op jit(solution)/shard_map/dynamic_update_slice | solution.py:124
  228.7 10.9 %reduce-scatter.5.cloned.1.call-done = f32[2,128,512]{2,1,0:T(8,128)} async-done(((f32[2,512,512]{2,1,0:T(8,128)}), f32[2,128,512]{2,1,0:T(8,128)}) %reduce-scatter.5.cloned.1.call-update) | async-done | bytes 524304 | tf_op jit(solution)/shard_map/reduce_scatter | solution.py:148
  241.1 6.6 %dynamic_update_slice.20 = f32[2,512,2048]{2,1,0:T(8,128)} dynamic-update-slice(f32[2,512,2048]{2,1,0:T(8,128)} %dynamic_update_slice.19, f32[2,128,512]{2,1,0:T(8,128)S(1)} %select_add_fusion.1, s32[]{:T(128)} %constant.98.clone.1, s32[]{:T(128)S(6)} %select_n.197, s32[]{:T(128)S(6)} %select_n.198) | dynamic-update-slice | bytes 1048580 | tf_op jit(solution)/shard_map/dynamic_update_slice | solution.py:124
  249.0 6.5 %dynamic_update_slice.21 = f32[2,512,2048]{2,1,0:T(8,128)} dynamic-update-slice(f32[2,512,2048]{2,1,0:T(8,128)} %dynamic_update_slice.20, f32[2,128,512]{2,1,0:T(8,128)S(1)} %select_add_fusion, s32[]{:T(128)} %constant.98.clone.1, s32[]{:T(128)S(6)} %select_n.200, s32[]{:T(128)S(6)} %select_n.198) | dynamic-update-slice | bytes 1048580 | tf_op jit(solution)/shard_map/dynamic_update_slice | solution.py:124
  255.5 42.8 %all-reduce.2.cloned.1.call-done = f32[2,128,512]{2,1,0:T(8,128)} async-done(((f32[2,128,512]{2,1,0:T(8,128)}), f32[2,128,512]{2,1,0:T(8,128)}) %all-reduce.2.cloned.1.call-update) | async-done | bytes 524304 | tf_op jit(solution)/shard_map/psum | solution.py:149
  300.2 89.5 %reduce-scatter.3.cloned.1.call-done = f32[2,4,128,256]{3,2,1,0:T(8,128)} async-done(((f32[2,4,128,2048]{3,2,1,0:T(8,128)}), f32[2,4,128,256]{3,2,1,0:T(8,128)}) %reduce-scatter.3.cloned.1.call-update) | async-done | bytes 1048592 | tf_op jit(solution)/shard_map/reduce_scatter | solution.py:150
  (89 shorter events, 48.5 us)
Async XLA Ops:
  7.2 53.0 %all-gather.2.cloned.1.call-start = ((), (), s32[]{:S(2)}) async-start(), calls=%async_computation.6 | async-start | bytes 4718592 | tf_op jit(solution)/shard_map/all_gather | solution.py:50
  84.8 15.5 %all-to-all-start = ((f32[2,512,128]{2,0,1:T(2,128)}), f32[2,512,128]{2,0,1:T(2,128)S(1)}, u32[]{:S(2)}, u32[]{:S(2)}) async-start(f32[2,512,128]{2,0,1:T(2,128)} %copy.38), calls=%async_computation | async-start | bytes 1048576 | tf_op jit(solution)/shard_map/all_to_all | solution.py:99
  100.3 16.6 %all-to-all-start.1 = ((f32[2,512,128]{2,0,1:T(2,128)}), f32[2,512,128]{2,0,1:T(2,128)S(1)}, u32[]{:S(2)}, u32[]{:S(2)}) async-start(f32[2,512,128]{2,0,1:T(2,128)} %copy.40), calls=%async_computation.1 | async-start | bytes 1048576 | tf_op jit(solution)/shard_map/all_to_all | solution.py:100
  117.4 13.3 %copy-start.2 = (f32[2,128,512]{2,1,0:T(8,128)S(1)}, f32[2,128,512]{2,1,0:T(8,128)}, u32[]{:S(2)}) copy-start(f32[2,128,512]{2,1,0:T(8,128)} %param.9) | copy-start | bytes 1572868
  123.8 12.0 %copy-start.3 = (f32[2,128,512]{2,1,0:T(8,128)}, f32[2,128,512]{2,1,0:T(8,128)S(1)}, u32[]{:S(2)}) copy-start(f32[2,128,512]{2,1,0:T(8,128)S(1)} %convolution_add_fusion.2) | copy-start | bytes 1572868
  130.7 5.1 %copy-start.5 = (f32[2,128,512]{2,1,0:T(8,128)}, f32[2,128,512]{2,1,0:T(8,128)S(1)}, u32[]{:S(2)}) copy-start(f32[2,128,512]{2,1,0:T(8,128)S(1)} %convolution_subtract_fusion.2) | copy-start | bytes 1572868
  141.7 16.7 %all-to-all-start.3 = ((f32[2,128,512]{1,0,2:T(2,128)}), f32[2,128,512]{1,0,2:T(2,128)S(1)}, u32[]{:S(2)}, u32[]{:S(2)}) async-start(f32[2,128,512]{1,0,2:T(2,128)} %copy.44), calls=%async_computation.3 | async-start | bytes 1048576 | tf_op jit(solution)/shard_map/all_to_all | solution.py:109
  146.1 6.3 %copy-start.4 = (f32[2,128,512]{2,1,0:T(8,128)S(1)}, f32[2,128,512]{2,1,0:T(8,128)}, u32[]{:S(2)}) copy-start(f32[2,128,512]{2,1,0:T(8,128)} %copy-done.3) | copy-start | bytes 1572868
  146.1 6.3 %copy-start.6 = (f32[2,128,512]{2,1,0:T(8,128)S(1)}, f32[2,128,512]{2,1,0:T(8,128)}, u32[]{:S(2)}) copy-start(f32[2,128,512]{2,1,0:T(8,128)} %copy-done.5) | copy-start | bytes 1572868
  158.5 15.1 %all-to-all-start.2 = ((f32[2,128,512]{1,0,2:T(2,128)}), f32[2,128,512]{1,0,2:T(2,128)S(1)}, u32[]{:S(2)}, u32[]{:S(2)}) async-start(f32[2,128,512]{1,0,2:T(2,128)} %copy.42), calls=%async_computation.2 | async-start | bytes 1048576 | tf_op jit(solution)/shard_map/all_to_all | solution.py:108
  162.7 77.0 %reduce-scatter.5.cloned.1.call-start = ((), (), s32[]{:S(2)}) async-start(), calls=%async_computation.8 | async-start | bytes 2621440 | tf_op jit(solution)/shard_map/reduce_scatter | solution.py:148
  167.6 6.0 %copy-start = (f32[2,512,128]{1,2,0:T(8,128)}, f32[2,512,128]{1,2,0:T(8,128)S(1)}, u32[]{:S(2)}) copy-start(f32[2,512,128]{1,2,0:T(8,128)S(1)} %all_to_all.67) | copy-start | bytes 1572868
  173.6 5.9 %copy-start.1 = (f32[2,512,128]{1,2,0:T(8,128)S(1)}, f32[2,512,128]{1,2,0:T(8,128)}, u32[]{:S(2)}) copy-start(f32[2,512,128]{1,2,0:T(8,128)} %copy-done) | copy-start | bytes 1572868
  174.2 11.0 %copy-start.7 = (f32[2,128,512]{2,1,0:T(8,128)S(1)}, f32[2,128,512]{2,1,0:T(8,128)}, u32[]{:S(2)}) copy-start(f32[2,128,512]{2,1,0:T(8,128)} %fusion.15) | copy-start | bytes 1572868
  205.6 92.7 %all-reduce.2.cloned.1.call-start = ((), (), s32[]{:S(2)}) async-start(), calls=%async_computation.9 | async-start | bytes 1048576 | tf_op jit(solution)/shard_map/psum | solution.py:149
  239.7 150.0 %reduce-scatter.3.cloned.1.call-start = ((), (), s32[]{:S(2)}) async-start(), calls=%async_computation.7 | async-start | bytes 9437184 | tf_op jit(solution)/shard_map/reduce_scatter | solution.py:150
Sparse Core Ops, SparseCore 0:
  9.6 50.4 all-gather.1
  205.7 33.9 reduce-scatter.4
  242.1 56.1 all-reduce.1
  301.0 88.5 reduce-scatter.2
where the time goes:
time: 403 us; the launch traced here: 397 us
  waiting for transfers between devices  186 us (46%)
  matrix products  89.4 us (22%)
  local copies, waits for them, and re-layouts  62.9 us (16%)
  between operations  24.9 us (6%)
  starting transfers between devices  16.9 us (4%)
  other arithmetic  15.7 us (4%)
    reduce_scatter x1, waiting for transfers between devices, on_device(): lax.psum_scatter(grad_band.reshape(2, cycles, rows_dev, full_width), 'sca...  89.5 us
    dot_general x16, matrix products, contract(): jnp.einsum(form, left_side, right_side, precision=lax.Precision.HIGHEST,...  89.4 us
    psum x1, waiting for transfers between devices, on_device(): probe_grad = lax.psum(probe_part, 'scan')  42.8 us
    all_gather x1, waiting for transfers between devices, on_device(): band_rows = lax.all_gather(object_slice, 'scan', axis=3, tiled=True)  42.2 us
    dynamic_update_slice x4, local copies, waits for them, and re-layouts, add_tile(): return lax.dynamic_update_slice(band_now, current + tile_value, corner)  22.6 us
    gather x12, local copies, waits for them, and re-layouts  12.3 us
    reduce_scatter x1, waiting for transfers between devices, on_device(): lax.psum_scatter(probe_full, 'depth', scatter_dimension=1, tiled=True)  10.9 us
  transfers between devices with their start and end apart: 8, of which 4 were waited for; matrix products, arithmetic and copies ran while one was open for 22% of the time, Pallas kernels for 0%

commit v1 on v0

v1 whole, which is shorter than its diff:
```python
import functools
import math

import jax
import jax.numpy as jnp
import ml_dtypes
import numpy as np
from jax import lax
from jax.experimental import pallas as pl
from jax.experimental.pallas import tpu as pltpu
from jax.sharding import PartitionSpec as P

fresnel_scale = 4
LANE = 128
SUB = 8
TOP = 32767.0
VMEM_LIMIT = 56 * 1024 * 1024


def split_table(table):
    high = table.astype(ml_dtypes.bfloat16)
    low = (table - high.astype(np.float32)).astype(ml_dtypes.bfloat16)
    return high, low


def dft_tables(size):
    index = np.arange(size)
    angle = 2.0 * math.pi / size * ((index[:, None] * index[None, :]) % size)
    re = np.cos(angle) / math.sqrt(size)
    im = -np.sin(angle) / math.sqrt(size)
    table = np.block([[re, im], [-im, re]]).astype(np.float32)
    return split_table(table), split_table(np.ascontiguousarray(table.T))


def chirp_vectors(size):
    index = np.arange(size)
    phase = (index - size // 2) ** 2 % (2 * fresnel_scale * size)
    angle = math.pi / (fresnel_scale * size) * phase
    return np.cos(angle).astype(np.float32), np.sin(angle).astype(np.float32)


def halves(x):
    high = x.astype(jnp.bfloat16)
    return high, (x - high.astype(jnp.float32)).astype(jnp.bfloat16)


def dot(a, b):
    return jnp.dot(a, b, preferred_element_type=jnp.float32)


def right_mix(x, high, low):
    x_high, x_low = halves(x)
    return dot(x_high, high[...]) + (dot(x_low, high[...]) + dot(x_high, low[...]))


def left_mix(high, low, x):
    x_high, x_low = halves(x)
    return dot(high[...], x_high) + (dot(high[...], x_low) + dot(low[...], x_high))


def factor_kernel(pos, rows, size, start, probe, row_cos, row_sin, col, chirp, pc, doubled):
    doubled[:, :size] = probe[...].astype(jnp.float32)
    doubled[:, size : 2 * size] = doubled[:, :size]
    doubled[:, 2 * size :] = jnp.zeros_like(doubled[:, 2 * size :])
    cc, cs = col[0:1, :], col[1:2, :]
    for p in range(pos):
        here = pl.ds(pl.multiple_of(start[p] // SUB * SUB, SUB), rows + SUB)
        turn = (rows + SUB - start[p] % SUB) % (rows + SUB)
        rc = pltpu.roll(row_cos[here, :], turn, 0)[:rows, 0:1]
        rs = pltpu.roll(row_sin[here, :], turn, 0)[:rows, 0:1]
        ch_re = rc * cc - rs * cs
        ch_im = rs * cc + rc * cs
        pr_re = pltpu.roll(doubled[0, here, :], turn, 0)[:rows]
        pr_im = pltpu.roll(doubled[1, here, :], turn, 0)[:rows]
        chirp[p, 0] = ch_re
        chirp[p, 1] = ch_im
        pc[p, 0] = pr_re * ch_re - pr_im * ch_im
        pc[p, 1] = pr_re * ch_im + pr_im * ch_re


def forward_kernel(pos, rows, size, depth, meta, band, pc, high, low, half, patch, psi):
    width = band.shape[2]
    span = size + LANE
    ids = lax.broadcasted_iota(jnp.int32, (rows, size), 0)
    for p in range(pos):
        first, second, left, cut = meta[p, 0], meta[p, 1], meta[p, 2], meta[p, 3]
        base = pl.multiple_of(jnp.minimum(left // LANE * LANE, width - span), LANE)
        turn = (span - (left - base)) % span
        for part in range(2):
            def tile(cycle):
                at = pl.multiple_of(cycle * rows, rows)
                raw = band[part, pl.ds(at, rows), pl.ds(base, span)].astype(jnp.float32)
                return pltpu.roll(raw, turn, 1)[:, :size]

            patch[p, part] = jnp.where(ids >= cut, tile(first), tile(second))
        o_re, o_im = patch[p, 0], patch[p, 1]
        here = pl.ds(p * rows, rows)
        psi[here, :size] = o_re * pc[p, 0] - o_im * pc[p, 1]
        psi[here, size:] = o_re * pc[p, 1] + o_im * pc[p, 0]
    out = right_mix(psi[...], high, low)
    block = size // depth
    for d in range(depth):
        for part in range(2):
            for p in range(pos):
                half[d, part, p] = out[
                    p * rows : (p + 1) * rows, part * size + d * block : part * size + (d + 1) * block
                ]


def middle_kernel(pos, rows, size, depth, half, data, fwd_high, fwd_low, inv_high, inv_low, mid, stack):
    block = size // depth
    for d in range(depth):
        for part in range(2):
            for p in range(pos):
                stack[part * size + d * rows : part * size + (d + 1) * rows,
                      p * block : (p + 1) * block] = half[d, part, p]
    far = left_mix(fwd_high, fwd_low, stack[...])
    re, im = far[:size], far[size:]
    excess = re * re + im * im - data[...]
    stack[:size] = excess * re
    stack[size:] = excess * im
    out = left_mix(inv_high, inv_low, stack[...])
    for d in range(depth):
        for part in range(2):
            for p in range(pos):
                mid[d, part, p] = out[part * size + d * rows : part * size + (d + 1) * rows,
                                      p * block : (p + 1) * block]


def turn_column(column, rows):
    eye = lax.broadcasted_iota(jnp.int32, (rows, rows), 0) == lax.broadcasted_iota(
        jnp.int32, (rows, rows), 1
    )
    return jnp.sum(jnp.where(eye, column, 0.0), axis=0, keepdims=True)


def turn_row(row, rows):
    eye = lax.broadcasted_iota(jnp.int32, (rows, rows), 0) == lax.broadcasted_iota(
        jnp.int32, (rows, rows), 1
    )
    return jnp.sum(jnp.where(eye, row, 0.0), axis=1, keepdims=True)


def backward_kernel(
    pos, rows, size, depth, start, mid, patch, pc, chirp, high, low, codes, scales, probe, stack, doubled
):
    block = size // depth
    for d in range(depth):
        for part in range(2):
            for p in range(pos):
                stack[p * rows : (p + 1) * rows,
                      part * size + d * block : part * size + (d + 1) * block] = mid[d, part, p]
    back = right_mix(stack[...], high, low)
    doubled[...] = jnp.zeros_like(doubled)
    for p in range(pos):
        b_re = back[p * rows : (p + 1) * rows, :size]
        b_im = back[p * rows : (p + 1) * rows, size:]
        c_re = pc[p, 0] * b_re + pc[p, 1] * b_im
        c_im = pc[p, 0] * b_im - pc[p, 1] * b_re
        for part, value in enumerate((c_re, c_im)):
            for b in range(size // LANE):
                lanes = slice(b * LANE, (b + 1) * LANE)
                piece = value[:, lanes]
                peak = jnp.max(jnp.abs(piece), axis=1, keepdims=True)
                safe = jnp.where(peak > 1e-30, peak, 1.0)
                coded = jnp.round(piece * (TOP / safe)).astype(jnp.int32)
                codes[p, part, :, lanes] = coded.astype(jnp.int16)
                scales[p, part, b : b + 1, :] = turn_column(safe * (1.0 / TOP), rows)
        g_re = b_re * chirp[p, 0] + b_im * chirp[p, 1]
        g_im = b_im * chirp[p, 0] - b_re * chirp[p, 1]
        o_re, o_im = patch[p, 0], patch[p, 1]
        here = pl.ds(pl.multiple_of(start[p] // SUB * SUB, SUB), rows + SUB)
        margin = jnp.zeros((SUB, size), jnp.float32)
        for part, value in enumerate((o_re * g_re + o_im * g_im, o_re * g_im - o_im * g_re)):
            tall = jnp.concatenate([value, margin], axis=0)
            doubled[part, here, :] += pltpu.roll(tall, start[p] % SUB, 0)
    probe[...] = doubled[:, :size] + doubled[:, size : 2 * size]


def place_kernel(groups, pos, rows, size, cols, meta, codes, scales, grad):
    grad[...] = jnp.zeros_like(grad)
    row_ids = lax.broadcasted_iota(jnp.int32, (rows, cols), 0)
    col_ids = lax.broadcasted_iota(jnp.int32, (rows, cols), 1)

    def slot(q, carry):
        g, p = q // pos, q % pos
        first, second, shift, cut = meta[q, 0], meta[q, 1], meta[q, 2], meta[q, 3]

        @pl.when(jnp.logical_and(shift > -cols, shift < size))
        def _():
            turn = (size - shift) % size
            inside = jnp.logical_and(col_ids + shift >= 0, col_ids + shift < size)
            take = row_ids >= cut
            for part in range(2):
                pieces = []
                for b in range(size // LANE):
                    raw = codes[g, p, part, :, b * LANE : (b + 1) * LANE].astype(jnp.int32)
                    unit = turn_row(scales[g, p, part, b : b + 1, :], rows)
                    pieces.append(raw.astype(jnp.float32) * unit)
                value = pltpu.roll(jnp.concatenate(pieces, axis=1), turn, 1)[:, :cols]
                value = jnp.where(inside, value, 0.0)
                grad[part, first] += jnp.where(take, value, 0.0)
                grad[part, second] += jnp.where(take, 0.0, value)

        return carry

    lax.fori_loop(0, groups * pos, slot, 0)


def call(kernel, outs, specs, scratch=(), flops=0, moved=0):
    return pl.pallas_call(
        kernel,
        out_shape=outs,
        in_specs=specs,
        out_specs=jax.tree.map(lambda _: pl.BlockSpec(memory_space=pltpu.VMEM), outs),
        scratch_shapes=list(scratch),
        compiler_params=pltpu.CompilerParams(vmem_limit_bytes=VMEM_LIMIT),
        cost_estimate=pl.CostEstimate(flops=flops, bytes_accessed=moved, transcendentals=0),
    )


def on_device(scan_size, depth_size, object_slice, probe_field, offsets, assignment, intensities):
    depth_index = lax.axis_index("depth")
    scan_index = lax.axis_index("scan")
    _, cycles, rows, cols = object_slice.shape
    size = probe_field.shape[2]
    pos = assignment.shape[0]
    block = size // depth_size
    f32 = jnp.float32
    vm = pl.BlockSpec(memory_space=pltpu.VMEM)
    sm = pl.BlockSpec(memory_space=pltpu.SMEM)
    (t_high, t_low), (u_high, u_low) = dft_tables(size)
    ch_cos, ch_sin = chirp_vectors(size)

    band = lax.all_gather(object_slice, "scan", axis=3, tiled=True)
    full = band.shape[3]
    band = band.reshape(2, cycles * rows, full)
    slots = lax.all_gather(assignment, "scan", axis=0, tiled=True)

    def describe(where):
        top, left = where[:, 0], where[:, 1]
        first = top // size
        second = jnp.minimum(first + 1, cycles - 1)
        cut = top % size - depth_index * rows
        return jnp.stack([first, second, left, cut], 1).astype(jnp.int32), top

    meta, top = describe(offsets[assignment])
    start = (depth_index * rows - top) % size
    meta_all, _ = describe(offsets[slots])
    meta_all = jnp.stack(
        [meta_all[:, 0], meta_all[:, 1], scan_index * cols - meta_all[:, 2], meta_all[:, 3]], 1
    )

    wide = jax.ShapeDtypeStruct((pos, 2, rows, size), f32)
    cut_shape = jax.ShapeDtypeStruct((depth_size, 2, pos, rows, block), f32)
    row_cos = np.ascontiguousarray(np.broadcast_to(np.resize(ch_cos, 2 * size + SUB)[:, None], (2 * size + SUB, LANE)))
    row_sin = np.ascontiguousarray(np.broadcast_to(np.resize(ch_sin, 2 * size + SUB)[:, None], (2 * size + SUB, LANE)))
    chirp, pc = call(
        functools.partial(factor_kernel, pos, rows, size),
        (wide, wide),
        [sm, vm, vm, vm, vm],
        [pltpu.VMEM((2, 2 * size + SUB, size), f32)],
        flops=10_000_000,
        moved=4_000_000,
    )(start, probe_field, row_cos, row_sin, np.stack([ch_cos, ch_sin]))
    data = intensities.transpose(2, 0, 1).reshape(size, pos * block)

    half, patch = call(
        functools.partial(forward_kernel, pos, rows, size, depth_size),
        (cut_shape, wide),
        [sm, vm, vm, vm, vm],
        [pltpu.VMEM((pos * rows, 2 * size), f32)],
    )(meta, band, pc, t_high, t_low)
    half = lax.all_to_all(half, "depth", split_axis=0, concat_axis=0, tiled=True)
    mid = call(
        functools.partial(middle_kernel, pos, rows, size, depth_size),
        cut_shape,
        [vm] * 6,
        [pltpu.VMEM((2 * size, pos * block), f32)],
    )(half, data, u_high, u_low, t_high, t_low)
    mid = lax.all_to_all(mid, "depth", split_axis=0, concat_axis=0, tiled=True)
    codes, scales, probe = call(
        functools.partial(backward_kernel, pos, rows, size, depth_size),
        (
            jax.ShapeDtypeStruct((pos, 2, rows, size), jnp.int16),
            jax.ShapeDtypeStruct((pos, 2, size // LANE, rows), f32),
            jax.ShapeDtypeStruct((2, size, size), f32),
        ),
        [sm, vm, vm, vm, vm, vm, vm],
        [pltpu.VMEM((pos * rows, 2 * size), f32), pltpu.VMEM((2, 2 * size + SUB, size), f32)],
    )(start, mid, patch, pc, chirp, u_high, u_low)

    all_codes = lax.all_gather(codes, "scan", axis=0, tiled=False)
    all_scales = lax.all_gather(scales, "scan", axis=0, tiled=False)
    probe_part = lax.psum_scatter(probe, "depth", scatter_dimension=1, tiled=True)
    probe_grad = lax.psum(probe_part, "scan") * (pos * scan_size) ** (-0.5)
    object_grad = call(
        functools.partial(place_kernel, scan_size, pos, rows, size, cols),
        jax.ShapeDtypeStruct((2, cycles, rows, cols), f32),
        [sm, vm, vm],
    )(meta_all, all_codes, all_scales)
    return object_grad, probe_grad


def solution(mesh):
    return jax.shard_map(
        functools.partial(on_device, mesh.shape["scan"], mesh.shape["depth"]),
        mesh=mesh,
        in_specs=(P(None, None, "depth", "scan"), P(), P(), P("scan"), P("scan", "depth", None)),
        out_specs=(P(None, None, "depth", "scan"), P(None, "depth", None)),
        check_vma=False,
    )
```

time: 403 us -> 231 us (0.57); the launches traced: 397 us -> 230 us
  waiting for transfers between devices: 186 us -> 81.6 us
  matrix products: 89.4 us -> 0 us
  blocking collectives: 0 us -> 84.8 us
  local copies, waits for them, and re-layouts: 62.9 us -> 5.24 us
  Pallas kernels: 0 us -> 35.6 us
  starting transfers between devices: 16.9 us -> 3.9 us
  other arithmetic: 15.7 us -> 4.57 us
  between operations: 24.9 us -> 14.5 us
    dot_general x16 -> x0, matrix products: 89.4 us -> none  [contract(): jnp.einsum(form, left_side, right_side, precision=lax.Precision.HIGHEST,...]
    reduce_scatter x2 -> x1, waiting for transfers between devices: 100 us -> 22.4 us  [on_device(): lax.psum_scatter(probe, 'depth', scatter_dimension=1, tiled=True)]
    all_gather x0 -> x2, blocking collectives: none -> 60.2 us  [the longest x1 44.7 us: on_device(): all_codes = lax.all_gather(codes, 'scan', axis=0, tiled=False)]
    psum x1, waiting for transfers between devices: 42.8 us -> 0.08 us  [on_device(): probe_grad = lax.psum(probe_part, 'scan') * (pos * scan_size) ** (-0.5)]
    pallas_call x0 -> x5, Pallas kernels: none -> 35.6 us  [the longest x1 11.6 us: on_device(): call(functools.partial(middle_kernel, pos, rows, size, depth_size), cut_s...]
    dynamic_update_slice x6 -> x0, local copies, waits for them, and re-layouts: 29.6 us -> none  [the longest x4 22.6 us: add_tile(): return lax.dynamic_update_slice(band_now, current + tile_value, corner)]
    all_to_all x0 -> x1, blocking collectives: none -> 18.1 us  [on_device(): mid = lax.all_to_all(mid, 'depth', split_axis=0, concat_axis=0, tiled=True)]
    gather x14 -> x2, local copies, waits for them, and re-layouts: 14.4 us -> 1.12 us  [the longest x1 0.56 us: on_device(): meta_all, _ = describe(offsets[slots])]
  transfers between devices with their start and end apart: 8 -> 4, of which waited for: 4 -> 4; matrix products, arithmetic and copies ran while one was open for 22% -> 3% of each run, Pallas kernels for 0% -> 4%
where the time goes in v1:
time: 231 us; the launch traced here: 230 us
  blocking collectives  84.8 us (37%)
  waiting for transfers between devices  81.6 us (35%)
  Pallas kernels  35.6 us (15%)
  between operations  14.5 us (6%)
  local copies, waits for them, and re-layouts  5.24 us (2%)
  other arithmetic  4.57 us (2%)
  starting transfers between devices  3.9 us (2%)
    all_gather x1, waiting for transfers between devices, on_device(): band = lax.all_gather(object_slice, 'scan', axis=3, tiled=True)  45.2 us
    all_gather x1, blocking collectives, on_device(): all_codes = lax.all_gather(codes, 'scan', axis=0, tiled=False)  44.7 us
    reduce_scatter x1, waiting for transfers between devices, on_device(): lax.psum_scatter(probe, 'depth', scatter_dimension=1, tiled=True)  22.4 us
    all_to_all x1, blocking collectives, on_device(): mid = lax.all_to_all(mid, 'depth', split_axis=0, concat_axis=0, tiled=True)  18.1 us
    all_gather x1, blocking collectives, on_device(): all_scales = lax.all_gather(scales, 'scan', axis=0, tiled=False)  15.5 us
    all_to_all x1, waiting for transfers between devices, on_device(): lax.all_to_all(half, 'depth', split_axis=0, concat_axis=0, tiled=True)  13.1 us
    pallas_call x1, Pallas kernels, on_device(): call(functools.partial(middle_kernel, pos, rows, size, depth_size), cut_s...  11.6 us
    pallas_call x1, Pallas kernels, on_device(): call(functools.partial(backward_kernel, pos, rows, size, depth_size), (ja...  8.14 us
  transfers between devices with their start and end apart: 4, of which 4 were waited for; matrix products, arithmetic and copies ran while one was open for 3% of the time, Pallas kernels for 4%

profile of v1, /device:TPU:0, one launch (start us, length us, event | category | flops | bytes accessed | tf_op | source)
XLA Modules:
  0.0 230.2 jit_solution(11867554584692477159)
XLA Ops:
  7.2 0.0 all-gather.5.cloned.1.call-start
  7.2 0.7 all-gather.5.cloned.1.call-update
  7.9 0.8 copy.28
  8.7 0.7 compare_select_fusion
  9.3 0.6 gather_fusion.1
  9.9 0.1 add_minimum_fusion.1
  10.0 0.5 and_select_fusion.2.start
  10.5 3.8 %shard_map.131 = (f32[2,2,128,512]{3,2,1,0:T(8,128)}, f32[2,2,128,512]{3,2,1,0:T(8,128)}) custom-call(s32[2]{0:T(128)} %and_select_fusion.2.start, bf16[2,512,512]{2,1,0:T(8,128)(2,1)} %probe.1, f32[1032,128]{1,0:T(8,128)} %constant.88.clone.row_cos, f32[1032,128]{1,0:T(8,128)} %constant.89.clone.row_sin, f32[2,512]{1,0:T(2,128)} %constant.90.clone.col), custom_call_target="tpu_custom_call" | custom-call | flops 10000000 | bytes 4000000 | tf_op jit(solution)/shard_map/pallas_call | solution.py:258
  14.3 0.6 pad_add_fusion.1.meta
  14.9 45.2 %all-gather.5.cloned.1.call-done = bf16[2,4,128,2048]{3,2,1,0:T(8,128)(2,1)} async-done(((bf16[2,4,128,256]{3,2,1,0:T(8,128)(2,1)}), bf16[2,4,128,2048]{3,2,1,0:T(8,128)(2,1)}) %all-gather.5.cloned.1.call-update) | async-done | bytes 4194320 | tf_op jit(solution)/shard_map/all_gather | solution.py:235
  60.1 7.2 %shard_map.132 = (f32[4,2,2,128,128]{4,3,2,1,0:T(8,128)}, f32[2,2,128,512]{3,2,1,0:T(8,128)}) custom-call(s32[2,4]{1,0:T(2,128)} %pad_add_fusion.1.meta, bf16[2,512,2048]{2,1,0:T(8,128)(2,1)} %bitcast.8, f32[2,2,128,512]{3,2,1,0:T(8,128)} %get-tuple-element.9.pc, bf16[1024,1024]{1,0:T(8,128)(2,1)} %constant.91.clone.high.inv_high, ...), custom_call_target="tpu_custom_call" | custom-call | tf_op jit(solution)/shard_map/pallas_call | solution.py:268
  67.4 3.8 %all-to-all-start = ((f32[4,2,2,128,128]{4,3,2,1,0:T(8,128)}), f32[4,2,2,128,128]{4,3,2,1,0:T(8,128)S(1)}, u32[]{:S(2)}, u32[]{:S(2)}) async-start(f32[4,2,2,128,128]{4,3,2,1,0:T(8,128)} %get-tuple-element.10), calls=%async_computation | async-start | bytes 2097152 | tf_op jit(solution)/shard_map/all_to_all | solution.py:274
  71.2 1.0 copy.31.data
  72.2 13.1 %all-to-all-done.half = f32[4,2,2,128,128]{4,3,2,1,0:T(8,128)S(1)} async-done(((f32[4,2,2,128,128]{4,3,2,1,0:T(8,128)}), f32[4,2,2,128,128]{4,3,2,1,0:T(8,128)S(1)}, u32[]{:S(2)}, u32[]{:S(2)}) %all-to-all-start) | async-done | bytes 1048608 | tf_op jit(solution)/shard_map/all_to_all | solution.py:274
  85.3 1.0 copy-done
  86.3 11.6 %shard_map.133 = f32[4,2,2,128,128]{4,3,2,1,0:T(8,128)} custom-call(f32[4,2,2,128,128]{4,3,2,1,0:T(8,128)} %copy-done, f32[512,256]{1,0:T(8,128)} %copy.31.data, bf16[1024,1024]{1,0:T(8,128)(2,1)} %constant.93.clone.fwd_high.high, bf16[1024,1024]{1,0:T(8,128)(2,1)} %constant.94.clone.fwd_low.low, bf16[1024,1024]{1,0:T(8,128)(2,1)} %constant.91.clone.high.inv_high, ...), custom_call_target="tpu_custom_call" | custom-call | tf_op jit(solution)/shard_map/pallas_call | solution.py:275
  97.9 18.1 %all_to_all.10.mid = f32[4,2,2,128,128]{4,3,2,1,0:T(8,128)} all-to-all(f32[4,2,2,128,128]{4,3,2,1,0:T(8,128)} %shard_map.133), channel_id=1, replica_groups=mesh['depth'=4,'scan'=8] {'depth'}, dimensions={0} | all-to-all | bytes 2097152 | tf_op jit(solution)/shard_map/all_to_all | solution.py:281
  116.0 8.1 %shard_map.134 = (s16[2,2,128,512]{3,2,1,0:T(8,128)(2,1)}, f32[2,2,4,128]{3,2,1,0:T(4,128)}, f32[2,512,512]{2,1,0:T(8,128)}) custom-call(s32[2]{0:T(128)} %and_select_fusion.2.start, f32[4,2,2,128,128]{4,3,2,1,0:T(8,128)} %all_to_all.10.mid, f32[2,2,128,512]{3,2,1,0:T(8,128)} %get-tuple-element.11.patch, f32[2,2,128,512]{3,2,1,0:T(8,128)} %get-tuple-element.9.pc, ...), custom_call_target="tpu_custom_call" | custom-call | tf_op jit(solution)/shard_map/pallas_call | solution.py:282
  124.2 0.0 all-reduce.3.cloned.1.call-start
  124.2 0.6 copy-done.5
  124.8 0.6 dynamic-slice
  126.1 0.2 dynamic-update-slice
  126.3 6.5 %all-reduce = s32[16]{0:T(128)S(1)} all-reduce(s32[16]{0:T(128)S(1)} %dynamic-update-slice), channel_id=1, replica_groups=mesh['depth'=4,'scan'=8] {'scan'}, use_global_device_ids=true, to_apply=%add | all-reduce | flops 16 | bytes 128
  132.8 0.6 gather_fusion
  133.4 0.1 slice_subtract_fusion
  133.5 0.7 pad_add_fusion.meta
  134.2 22.4 %reduce-scatter.2.cloned.1.call-done = f32[2,128,512]{2,1,0:T(8,128)} async-done(((f32[2,512,512]{2,1,0:T(8,128)}), f32[2,128,512]{2,1,0:T(8,128)}) %reduce-scatter.2.cloned.1.call-update) | async-done | bytes 524304 | tf_op jit(solution)/shard_map/reduce_scatter | solution.py:295
  156.6 44.7 %all-gather.6 = s16[16,2,128,512]{3,2,1,0:T(8,128)(2,1)} all-gather(s16[2,2,128,512]{3,2,1,0:T(8,128)(2,1)S(1)} %copy-done.1), channel_id=2, replica_groups=mesh['depth'=4,'scan'=8] {'scan'}, dimensions={0}, use_global_device_ids=true | all-gather | bytes 4718592 | tf_op jit(solution)/shard_map/all_gather | solution.py:293
  201.3 15.5 %all-gather.1 = f32[16,2,4,128]{3,2,1,0:T(4,128)} all-gather(f32[2,2,4,128]{3,2,1,0:T(4,128)S(1)} %copy-done.3), channel_id=3, replica_groups=mesh['depth'=4,'scan'=8] {'scan'}, dimensions={0}, use_global_device_ids=true | all-gather | bytes 73728 | tf_op jit(solution)/shard_map/all_gather | solution.py:294
  216.9 4.8 %shard_map.135 = f32[2,4,128,256]{3,2,1,0:T(8,128)} custom-call(s32[16,4]{1,0:T(8,128)} %pad_add_fusion.meta, s16[8,2,2,128,512]{4,3,2,1,0:T(8,128)(2,1)} %bitcast.7, f32[8,2,2,4,128]{4,3,2,1,0:T(4,128)} %bitcast.10), custom_call_target="tpu_custom_call" | custom-call | tf_op jit(solution)/shard_map/pallas_call | solution.py:297
  221.7 0.1 all-reduce.3.cloned.1.call-done
  221.8 1.9 broadcast_multiply_fusion
  (18 shorter events, 0.1 us)
Async XLA Ops:
  7.2 53.0 %all-gather.5.cloned.1.call-start = ((), (), s32[]{:S(2)}) async-start(), calls=%async_computation.3 | async-start | bytes 4718592 | tf_op jit(solution)/shard_map/all_gather | solution.py:235
  67.4 3.8 %copy-start.2 = (f32[2,128,512]{2,1,0:T(8,128)S(1)}, f32[2,128,512]{2,1,0:T(8,128)}, u32[]{:S(2)}) copy-start(f32[2,128,512]{2,1,0:T(8,128)} %param.16) | copy-start | bytes 1572868
  67.4 18.0 %all-to-all-start = ((f32[4,2,2,128,128]{4,3,2,1,0:T(8,128)}), f32[4,2,2,128,128]{4,3,2,1,0:T(8,128)S(1)}, u32[]{:S(2)}, u32[]{:S(2)}) async-start(f32[4,2,2,128,128]{4,3,2,1,0:T(8,128)} %get-tuple-element.10), calls=%async_computation | async-start | bytes 2097152 | tf_op jit(solution)/shard_map/all_to_all | solution.py:274
  71.2 85.4 %reduce-scatter.2.cloned.1.call-start = ((), (), s32[]{:S(2)}) async-start(), calls=%async_computation.4 | async-start | bytes 2621440 | tf_op jit(solution)/shard_map/reduce_scatter | solution.py:295
  85.3 1.0 copy-start
  124.1 0.7 copy-start.5
  124.1 1.9 copy-start.4
  124.2 32.5 %copy-start.1 = (s16[2,2,128,512]{3,2,1,0:T(8,128)(2,1)S(1)}, s16[2,2,128,512]{3,2,1,0:T(8,128)(2,1)}, u32[]{:S(2)}) copy-start(s16[2,2,128,512]{3,2,1,0:T(8,128)(2,1)} %get-tuple-element.13) | copy-start | bytes 1572868
  124.2 97.6 %all-reduce.3.cloned.1.call-start = ((), (), s32[]{:S(2)}) async-start(), calls=%async_computation.5 | async-start | bytes 1048576 | tf_op jit(solution)/shard_map/psum | solution.py:296
  156.6 44.7 %copy-start.3 = (f32[2,2,4,128]{3,2,1,0:T(4,128)S(1)}, f32[2,2,4,128]{3,2,1,0:T(4,128)}, u32[]{:S(2)}) copy-start(f32[2,2,4,128]{3,2,1,0:T(4,128)} %get-tuple-element.14) | copy-start | bytes 24580
Sparse Core Ops, SparseCore 0:
  9.6 50.4 all-gather.4
  124.3 32.2 reduce-scatter.1
  159.1 62.6 all-reduce.2

commit v2 on v1

v2 whole, which is shorter than its diff:
```python
import functools
import math

import jax
import jax.numpy as jnp
import ml_dtypes
import numpy as np
from jax import lax
from jax.experimental import pallas as pl
from jax.experimental.pallas import tpu as pltpu
from jax.sharding import PartitionSpec as P

fresnel_scale = 4
LANE = 128
SUB = 8
TOP = 32767.0
VMEM_LIMIT = 56 * 1024 * 1024


def split_table(table):
    high = table.astype(ml_dtypes.bfloat16)
    low = (table - high.astype(np.float32)).astype(ml_dtypes.bfloat16)
    return high, low


def dft_tables(size, depth):
    index = np.arange(size)
    angle = 2.0 * math.pi / size * ((index[:, None] * index[None, :]) % size)
    re = np.cos(angle) / math.sqrt(size)
    im = -np.sin(angle) / math.sqrt(size)
    table = np.block([[re, im], [-im, re]]).astype(np.float32)
    by_row = table.reshape(2, depth, size // depth, 2 * size).transpose(1, 0, 2, 3)
    by_row = by_row.reshape(depth, 2 * size // depth, 2 * size)
    by_col = table.reshape(2 * size, 2, depth, size // depth).transpose(2, 0, 1, 3)
    by_col = by_col.reshape(depth, 2 * size, 2 * size // depth)
    return split_table(np.ascontiguousarray(by_row)), split_table(np.ascontiguousarray(by_col))


def chirp_vectors(size):
    index = np.arange(size)
    phase = (index - size // 2) ** 2 % (2 * fresnel_scale * size)
    angle = math.pi / (fresnel_scale * size) * phase
    return np.cos(angle).astype(np.float32), np.sin(angle).astype(np.float32)


def halves(x):
    high = x.astype(jnp.bfloat16)
    return high, (x - high.astype(jnp.float32)).astype(jnp.bfloat16)


def dot(a, b):
    return jnp.dot(a, b, preferred_element_type=jnp.float32)


def right_mix(x, high, low):
    x_high, x_low = halves(x)
    return dot(x_high, high) + (dot(x_low, high) + dot(x_high, low))


def left_mix(high, low, x):
    x_high, x_low = halves(x)
    return dot(high, x_high) + (dot(high, x_low) + dot(low, x_high))


MESH = pl.DeviceIdType.MESH


def send(src, dst, send_sem, recv_sem, axis, target):
    return pltpu.make_async_remote_copy(
        src_ref=src, dst_ref=dst, send_sem=send_sem, recv_sem=recv_sem,
        device_id={axis: target}, device_id_type=MESH,
    )


class Gather:
    def __init__(self, scan, pairs, sems):
        self.scan, self.chips = scan, scan // 2
        self.me = lax.axis_index("scan")
        self.chip, self.core = self.me // 2, self.me % 2
        self.other = self.me + 1 - 2 * self.core
        self.pairs = pairs
        self.up_sem, self.down_sem, self.side_sem, self.recv_sem, self.own_sem = sems

    def has(self, shift):
        return jnp.logical_and(self.chip + shift >= 0, self.chip + shift < self.chips)

    def greet(self, barrier):
        for shift in (-1, 1):
            @pl.when(self.has(shift))
            def _():
                pl.semaphore_signal(
                    barrier, inc=1, device_id={"scan": self.me + 2 * shift}, device_id_type=MESH
                )
        pl.semaphore_signal(barrier, inc=1, device_id={"scan": self.other}, device_id_type=MESH)
        ends = jnp.where(self.chip == 0, 1, 0) + jnp.where(self.chip == self.chips - 1, 1, 0)
        return 3 - ends

    def moves(self, block, way, source=None):
        sem, target = {
            "up": (self.up_sem, self.me + 2),
            "down": (self.down_sem, self.me - 2),
            "side": (self.side_sem, self.other),
        }[way]
        return [
            send(out.at[block] if source is None else source[i], out.at[block],
                 sem.at[i, block], self.recv_sem.at[i, block], "scan", target)
            for i, (_, out) in enumerate(self.pairs)
        ]

    def start(self):
        own = [ref for ref, _ in self.pairs]
        for shift, way in ((1, "up"), (-1, "down")):
            @pl.when(self.has(shift))
            def _():
                for move in self.moves(self.me, way, own):
                    move.start()
        for move in self.moves(self.me, "side", own):
            move.start()
        for i, (ref, out) in enumerate(self.pairs):
            pltpu.make_async_copy(ref, out.at[self.me], self.own_sem.at[i]).start()

    def step(self, t):
        for shift, way in ((-1, "up"), (1, "down")):
            @pl.when(self.has(shift * t))
            def _():
                block = self.me + 2 * shift * t
                for move in self.moves(block, "side"):
                    move.wait_recv()

                @pl.when(self.has(-shift))
                def _():
                    for move in self.moves(block, way):
                        move.start()

                for move in self.moves(block, "side"):
                    move.start()

    def finish(self):
        for t in range(self.chips):
            for shift in (-1, 1) if t else (0,):
                @pl.when(self.has(shift * t))
                def _():
                    block = self.other + 2 * shift * t
                    for move in self.moves(block, "side"):
                        move.wait_recv()
                    mine = self.me + 2 * shift * t
                    for move in self.moves(mine, "side"):
                        move.wait_send()
        for i, (ref, out) in enumerate(self.pairs):
            pltpu.make_async_copy(ref, out.at[self.me], self.own_sem.at[i]).wait()
        for shift, way in ((-1, "up"), (1, "down")):
            @pl.when(self.has(-shift))
            def _():
                for t in range(self.chips):
                    @pl.when(self.has(shift * t))
                    def _():
                        for move in self.moves(self.me + 2 * shift * t, way):
                            move.wait_send()


def gather_sems(scan, count):
    dma = pltpu.SemaphoreType.DMA
    return [dma((count, scan))] * 4 + [dma((count,))]


def band_kernel(scan, block, band, *sems):
    gather = Gather(scan, [(block, band)], sems)
    barrier = pltpu.get_barrier_semaphore()
    pl.semaphore_wait(barrier, gather.greet(barrier))
    gather.start()
    for t in range(1, gather.chips):
        gather.step(t)
    gather.finish()


def tail_kernel(
    scan, depth, block, codes, aux, probe, all_codes, all_aux, result,
    land, acc, near, below, above, up_out, down_out, final, *sems
):
    gather = Gather(scan, [(codes, all_codes), (aux, all_aux)], sems[:5])
    d_send, d_recv, near_sem, up_sem, down_sem, final_sem = sems[5:]
    me = lax.axis_index("depth")
    barrier = pltpu.get_barrier_semaphore()
    partners = [lax.rem(me + i, depth) for i in range(1, depth)]
    sources = [lax.rem(me + depth - i, depth) for i in range(1, depth)]
    for e in partners:
        pl.semaphore_signal(barrier, inc=1, device_id={"depth": e}, device_id_type=MESH)
    pl.semaphore_wait(barrier, gather.greet(barrier) + (depth - 1))
    gather.start()
    parts = [send(probe.at[e], land.at[me], d_send.at[e], d_recv.at[me], "depth", e) for e in partners]
    for copy in parts:
        copy.start()
    gather.step(1)
    total = probe[me]
    for e in sources:
        send(probe.at[e], land.at[e], d_send.at[e], d_recv.at[e], "depth", e).wait_recv()
        total = total + land[e]
    acc[...] = total
    core = gather.core
    cross = send(acc.at[1 - core], near, near_sem.at[0], near_sem.at[1], "scan", gather.other)
    cross.start()
    for t in range(2, gather.chips - 1):
        gather.step(t)
    cross.wait_recv()
    up = send(up_out, below, up_sem.at[0], up_sem.at[1], "scan", gather.me + 2)
    down = send(down_out, above, down_sem.at[0], down_sem.at[1], "scan", gather.me - 2)
    mine = acc[core] + near[...]
    final[core] = mine
    up_out[...] = mine
    down_out[...] = mine

    @pl.when(gather.chip == 0)
    def _():
        up.start()

    @pl.when(gather.chip == gather.chips - 1)
    def _():
        down.start()

    def pass_up():
        @pl.when(gather.has(-1))
        def _():
            up.wait_recv()
            up_out[...] += below[...]
            final[core] += below[...]

            @pl.when(gather.has(1))
            def _():
                up.start()

    def pass_down():
        @pl.when(gather.has(1))
        def _():
            down.wait_recv()
            down_out[...] += above[...]
            final[core] += above[...]

            @pl.when(gather.has(-1))
            def _():
                down.start()

    low_half = 2 * gather.chip < gather.chips

    @pl.when(low_half)
    def _():
        pass_up()
        pass_down()

    @pl.when(jnp.logical_not(low_half))
    def _():
        pass_down()
        pass_up()

    last = send(final.at[core], final.at[core], final_sem.at[0], final_sem.at[1], "scan", gather.other)
    last.start()
    if gather.chips > 2:
        gather.step(gather.chips - 1)
    send(final.at[1 - core], final.at[1 - core], final_sem.at[0], final_sem.at[1], "scan",
         gather.other).wait_recv()
    result[...] = final[...]
    gather.finish()
    last.wait_send()
    cross.wait_send()
    for copy in parts:
        copy.wait_send()

    @pl.when(gather.has(1))
    def _():
        up.wait_send()

    @pl.when(gather.has(-1))
    def _():
        down.wait_send()


def wave_kernel(
    pos, rows, size, depth, psi, data, row_high, row_low, col_high, col_low, back,
    out1, land1, out2, land2, far, resid, send1, recv1, send2, recv2
):
    me = lax.axis_index("depth")
    block = size // depth
    partners = [lax.rem(me + i, depth) for i in range(1, depth)]
    sources = [lax.rem(me + depth - i, depth) for i in range(1, depth)]
    barrier = pltpu.get_barrier_semaphore()
    for e in partners:
        pl.semaphore_signal(barrier, inc=1, device_id={"depth": e}, device_id_type=MESH)
    pl.semaphore_wait(barrier, depth - 1)

    def to_rows(chunk, count, side):
        re = [chunk[p * count : (p + 1) * count, :side] for p in range(pos)]
        im = [-chunk[p * count : (p + 1) * count, side:] for p in range(pos)]
        return jnp.concatenate([jnp.concatenate(re, 1), jnp.concatenate(im, 1)], 0)

    def to_lanes(chunk, count, side):
        lines = [
            jnp.concatenate(
                [chunk[:count, p * side : (p + 1) * side], -chunk[count:, p * side : (p + 1) * side]], 1
            )
            for p in range(pos)
        ]
        return jnp.concatenate(lines, 0)

    wave_high, wave_low = halves(psi[...])

    def forward(e):
        high, low = col_high[e], col_low[e]
        return dot(wave_high, high) + (dot(wave_low, high) + dot(wave_high, low))

    copies = []
    for e in partners:
        out1[e] = forward(e)
        copy = send(out1.at[e], land1.at[me], send1.at[e], recv1.at[me], "depth", e)
        copy.start()
        copies.append(copy)
    far[...] = left_mix(col_high[me], col_low[me], to_rows(forward(me), rows, block))
    for e in sources:
        send(out1.at[e], land1.at[e], send1.at[e], recv1.at[e], "depth", e).wait_recv()
        far[...] += left_mix(col_high[e], col_low[e], to_rows(land1[e], rows, block))
    re, im = far[:size], far[size:]
    excess = re * re + im * im - data[...]
    resid[:size] = excess * re
    resid[size:] = -(excess * im)
    res_high, res_low = halves(resid[...])

    def middle(e):
        high, low = row_high[e], row_low[e]
        return dot(high, res_high) + (dot(high, res_low) + dot(low, res_high))

    for e in partners:
        out2[e] = middle(e)
        copy = send(out2.at[e], land2.at[me], send2.at[e], recv2.at[me], "depth", e)
        copy.start()
        copies.append(copy)
    back[...] = right_mix(to_lanes(middle(me), rows, block), row_high[me], row_low[me])
    for e in sources:
        send(out2.at[e], land2.at[e], send2.at[e], recv2.at[e], "depth", e).wait_recv()
        back[...] += right_mix(to_lanes(land2[e], rows, block), row_high[e], row_low[e])
    for copy in copies:
        copy.wait_send()


def factor_kernel(pos, rows, size, start, probe, row_cos, row_sin, col, chirp, pc, doubled):
    doubled[:, :size] = probe[...].astype(jnp.float32)
    doubled[:, size : 2 * size] = doubled[:, :size]
    doubled[:, 2 * size :] = jnp.zeros_like(doubled[:, 2 * size :])
    cc, cs = col[0:1, :], col[1:2, :]
    for p in range(pos):
        here = pl.ds(pl.multiple_of(start[p] // SUB * SUB, SUB), rows + SUB)
        turn = (rows + SUB - start[p] % SUB) % (rows + SUB)
        rc = pltpu.roll(row_cos[here, :], turn, 0)[:rows, 0:1]
        rs = pltpu.roll(row_sin[here, :], turn, 0)[:rows, 0:1]
        ch_re = rc * cc - rs * cs
        ch_im = rs * cc + rc * cs
        pr_re = pltpu.roll(doubled[0, here, :], turn, 0)[:rows]
        pr_im = pltpu.roll(doubled[1, here, :], turn, 0)[:rows]
        chirp[p, 0] = ch_re
        chirp[p, 1] = ch_im
        pc[p, 0] = pr_re * ch_re - pr_im * ch_im
        pc[p, 1] = pr_re * ch_im + pr_im * ch_re


def window_kernel(pos, rows, size, cols, scan, meta, band, pc, patch, psi):
    count = -(-(size + cols) // LANE) * LANE // cols
    span = count * cols
    ids = lax.broadcasted_iota(jnp.int32, (rows, size), 0)
    for p in range(pos):
        first, second, left, cut = meta[p, 0], meta[p, 1], meta[p, 2], meta[p, 3]
        turn = (span - left % cols) % span
        for part in range(2):
            def tile(cycle):
                raw = [
                    band[jnp.minimum(left // cols + i, scan - 1), part, cycle].astype(jnp.float32)
                    for i in range(count)
                ]
                return pltpu.roll(jnp.concatenate(raw, 1), turn, 1)[:, :size]

            patch[p, part] = jnp.where(ids >= cut, tile(first), tile(second))
        o_re, o_im = patch[p, 0], patch[p, 1]
        here = pl.ds(p * rows, rows)
        psi[here, :size] = o_re * pc[p, 0] - o_im * pc[p, 1]
        psi[here, size:] = o_re * pc[p, 1] + o_im * pc[p, 0]


def turn_column(column, rows):
    eye = lax.broadcasted_iota(jnp.int32, (rows, rows), 0) == lax.broadcasted_iota(
        jnp.int32, (rows, rows), 1
    )
    return jnp.sum(jnp.where(eye, column, 0.0), axis=0, keepdims=True)


def turn_row(row, rows):
    eye = lax.broadcasted_iota(jnp.int32, (rows, rows), 0) == lax.broadcasted_iota(
        jnp.int32, (rows, rows), 1
    )
    return jnp.sum(jnp.where(eye, row, 0.0), axis=1, keepdims=True)


def grad_kernel(
    pos, rows, size, depth, start, place, back, patch, pc, chirp, codes, aux, probe, doubled
):
    block = size // depth
    doubled[...] = jnp.zeros_like(doubled)
    for p in range(pos):
        b_re = back[p * rows : (p + 1) * rows, :size]
        b_im = -back[p * rows : (p + 1) * rows, size:]
        c_re = pc[p, 0] * b_re + pc[p, 1] * b_im
        c_im = pc[p, 0] * b_im - pc[p, 1] * b_re
        for part, value in enumerate((c_re, c_im)):
            for b in range(size // LANE):
                lanes = slice(b * LANE, (b + 1) * LANE)
                piece = value[:, lanes]
                peak = jnp.max(jnp.abs(piece), axis=1, keepdims=True)
                safe = jnp.where(peak > 1e-30, peak, 1.0)
                coded = jnp.round(piece * (TOP / safe)).astype(jnp.int32)
                codes[p, part, :, lanes] = coded.astype(jnp.int16)
                line = part * (size // LANE) + b
                aux[p, line : line + 1, :] = turn_column(safe * (1.0 / TOP), rows)
        lines = 2 * (size // LANE)
        aux[p, lines:, :] = jnp.zeros((SUB, rows), jnp.float32)
        for i in range(2):
            aux[p, lines + i : lines + i + 1, :] = jnp.full((1, rows), place[p, i], jnp.float32)
        g_re = b_re * chirp[p, 0] + b_im * chirp[p, 1]
        g_im = b_im * chirp[p, 0] - b_re * chirp[p, 1]
        o_re, o_im = patch[p, 0], patch[p, 1]
        here = pl.ds(pl.multiple_of(start[p] // SUB * SUB, SUB), rows + SUB)
        margin = jnp.zeros((SUB, size), jnp.float32)
        for part, value in enumerate((o_re * g_re + o_im * g_im, o_re * g_im - o_im * g_re)):
            tall = jnp.concatenate([value, margin], axis=0)
            doubled[part, here, :] += pltpu.roll(tall, start[p] % SUB, 0)
    for d in range(depth):
        low, high = d * block, (d + 1) * block
        probe[d] = doubled[:, low:high] + doubled[:, size + low : size + high]


def place_kernel(groups, pos, rows, size, cols, meta, codes, aux, grad):
    grad[...] = jnp.zeros_like(grad)
    row_ids = lax.broadcasted_iota(jnp.int32, (rows, cols), 0)
    col_ids = lax.broadcasted_iota(jnp.int32, (rows, cols), 1)

    def slot(q, carry):
        g, p = q // pos, q % pos
        first, second, shift, cut = meta[q, 0], meta[q, 1], meta[q, 2], meta[q, 3]

        @pl.when(jnp.logical_and(shift > -cols, shift < size))
        def _():
            turn = (size - shift) % size
            inside = jnp.logical_and(col_ids + shift >= 0, col_ids + shift < size)
            take = row_ids >= cut
            for part in range(2):
                pieces = []
                for b in range(size // LANE):
                    raw = codes[g, p, part, :, b * LANE : (b + 1) * LANE].astype(jnp.int32)
                    line = part * (size // LANE) + b
                    unit = turn_row(aux[g, p, line : line + 1, :], rows)
                    pieces.append(raw.astype(jnp.float32) * unit)
                value = pltpu.roll(jnp.concatenate(pieces, axis=1), turn, 1)[:, :cols]
                value = jnp.where(inside, value, 0.0)
                grad[part, first] += jnp.where(take, value, 0.0)
                grad[part, second] += jnp.where(take, 0.0, value)

        return carry

    lax.fori_loop(0, groups * pos, slot, 0)


def call(kernel, outs, specs, scratch=(), collective=None, out_specs=None):
    vm = pl.BlockSpec(memory_space=pltpu.VMEM)
    return pl.pallas_call(
        kernel,
        out_shape=outs,
        in_specs=specs,
        out_specs=out_specs or jax.tree.map(lambda _: vm, outs),
        scratch_shapes=list(scratch),
        compiler_params=pltpu.CompilerParams(
            vmem_limit_bytes=VMEM_LIMIT,
            collective_id=collective,
            has_side_effects=collective is not None,
        ),
    )


def on_device(scan_size, depth_size, object_slice, probe_field, offsets, assignment, intensities):
    depth_index = lax.axis_index("depth")
    scan_index = lax.axis_index("scan")
    _, cycles, rows, cols = object_slice.shape
    size = probe_field.shape[2]
    pos = assignment.shape[0]
    block = size // depth_size
    f32 = jnp.float32
    shape = jax.ShapeDtypeStruct
    vm = pl.BlockSpec(memory_space=pltpu.VMEM)
    sm = pl.BlockSpec(memory_space=pltpu.SMEM)
    hbm = pl.BlockSpec(memory_space=pl.ANY)
    dma = pltpu.SemaphoreType.DMA
    (row_high, row_low), (col_high, col_low) = dft_tables(size, depth_size)
    ch_cos, ch_sin = chirp_vectors(size)

    def describe(top, left):
        first = top // size
        second = jnp.minimum(first + 1, cycles - 1)
        cut = top % size - depth_index * rows
        return jnp.stack([first, second, left, cut], 1).astype(jnp.int32)

    place = offsets[assignment]
    top, left = place[:, 0], place[:, 1]
    meta = describe(top, left)
    start = (depth_index * rows - top) % size

    wide = shape((pos, 2, rows, size), f32)
    tall = 2 * size + SUB
    row_cos = np.ascontiguousarray(np.broadcast_to(np.resize(ch_cos, tall)[:, None], (tall, LANE)))
    row_sin = np.ascontiguousarray(np.broadcast_to(np.resize(ch_sin, tall)[:, None], (tall, LANE)))
    chirp, pc = call(
        functools.partial(factor_kernel, pos, rows, size),
        (wide, wide),
        [sm, vm, vm, vm, vm],
        [pltpu.VMEM((2, tall, size), f32)],
    )(start, probe_field, row_cos, row_sin, np.stack([ch_cos, ch_sin]))
    data = intensities.transpose(2, 0, 1).reshape(size, pos * block)

    band = call(
        functools.partial(band_kernel, scan_size),
        shape((scan_size,) + object_slice.shape, object_slice.dtype),
        [hbm],
        gather_sems(scan_size, 1),
        collective=0,
        out_specs=hbm,
    )(object_slice)
    patch, psi = call(
        functools.partial(window_kernel, pos, rows, size, cols, scan_size),
        (wide, shape((pos * rows, 2 * size), f32)),
        [sm, vm, vm],
    )(meta, band, pc)
    chunk = pltpu.VMEM((depth_size, pos * rows, 2 * block), f32)
    turned = pltpu.VMEM((depth_size, 2 * rows, pos * block), f32)
    tower = pltpu.VMEM((2 * size, pos * block), f32)
    back = call(
        functools.partial(wave_kernel, pos, rows, size, depth_size),
        shape((pos * rows, 2 * size), f32),
        [vm] * 6,
        [chunk, chunk, turned, turned, tower, tower] + [dma((depth_size,))] * 4,
        collective=1,
    )(psi, data, row_high, row_low, col_high, col_low)
    lines = 2 * (size // LANE) + SUB
    codes, aux, probe = call(
        functools.partial(grad_kernel, pos, rows, size, depth_size),
        (
            shape((pos, 2, rows, size), jnp.int16),
            shape((pos, lines, rows), f32),
            shape((depth_size, 2, block, size), f32),
        ),
        [sm, sm, vm, vm, vm, vm],
        [pltpu.VMEM((2, tall, size), f32)],
    )(start, place.astype(f32), back, patch, pc, chirp)
    slab = pltpu.VMEM((block, size), f32)
    pair = pltpu.VMEM((2, block, size), f32)
    all_codes, all_aux, probe_sum = call(
        functools.partial(tail_kernel, scan_size, depth_size, block),
        (
            shape((scan_size,) + codes.shape, codes.dtype),
            shape((scan_size,) + aux.shape, aux.dtype),
            shape((2, block, size), f32),
        ),
        [hbm, hbm, vm],
        [pltpu.VMEM((depth_size, 2, block, size), f32), pair, slab, slab, slab, slab, slab, pair]
        + gather_sems(scan_size, 2)
        + [dma((depth_size,))] * 2
        + [dma((2,))] * 4,
        collective=2,
        out_specs=(hbm, hbm, vm),
    )(codes, aux, probe)
    spots = all_aux[:, :, lines - SUB : lines - SUB + 2, 0].astype(jnp.int32).reshape(-1, 2)
    meta_all = describe(spots[:, 0], scan_index * cols - spots[:, 1])
    object_grad = call(
        functools.partial(place_kernel, scan_size, pos, rows, size, cols),
        shape((2, cycles, rows, cols), f32),
        [sm, vm, vm],
    )(meta_all, all_codes, all_aux)
    return object_grad, probe_sum * (pos * scan_size) ** (-0.5)


def solution(mesh):
    return jax.shard_map(
        functools.partial(on_device, mesh.shape["scan"], mesh.shape["depth"]),
        mesh=mesh,
        in_specs=(P(None, None, "depth", "scan"), P(), P(), P("scan"), P("scan", "depth", None)),
        out_specs=(P(None, None, "depth", "scan"), P(None, "depth", None)),
        check_vma=False,
    )
```

time: 231 us -> 163 us (0.71)
  Pallas kernels: 35.6 us -> 152 us
  blocking collectives: 84.8 us -> 0 us
  waiting for transfers between devices: 81.6 us -> 0 us
  between operations: 14.5 us -> 0.7 us
  starting transfers between devices: 3.9 us -> 0 us
    pallas_call x4 -> x6, Pallas kernels: 31.8 us -> 149 us  [the longest x1 50.9 us: on_device(): call(functools.partial(tail_kernel, scan_size, depth_size, block), (shape...]
    all_gather x2 -> x0, blocking collectives: 60.2 us -> none  [the longest x1 44.7 us: on_device(): all_codes = lax.all_gather(codes, 'scan', axis=0, tiled=False)]
    all_gather x1 -> x0, waiting for transfers between devices: 45.2 us -> none  [on_device(): band = lax.all_gather(object_slice, 'scan', axis=3, tiled=True)]
    reduce_scatter x1 -> x0, waiting for transfers between devices: 22.4 us -> none  [on_device(): lax.psum_scatter(probe, 'depth', scatter_dimension=1, tiled=True)]
    all_to_all x1 -> x0, blocking collectives: 18.1 us -> none  [on_device(): mid = lax.all_to_all(mid, 'depth', split_axis=0, concat_axis=0, tiled=True)]
    all_to_all x1 -> x0, waiting for transfers between devices: 13.1 us -> none  [on_device(): lax.all_to_all(half, 'depth', split_axis=0, concat_axis=0, tiled=True)]
    unnamed x1 -> x0, blocking collectives: 6.5 us -> none
    all_to_all x1 -> x0, starting transfers between devices: 3.82 us -> none  [on_device(): lax.all_to_all(half, 'depth', split_axis=0, concat_axis=0, tiled=True)]
  transfers between devices with their start and end apart: 4 -> 0, of which waited for: 4 -> 0; matrix products, arithmetic and copies ran while one was open for 3% -> 0% of each run, Pallas kernels for 4% -> 0%
where the time goes in v2:
time: 163 us; the launch traced here: 161 us
  Pallas kernels  152 us (93%)
  other arithmetic  4.65 us (3%)
  local copies, waits for them, and re-layouts  3.23 us (2%)
    pallas_call x1, Pallas kernels, on_device(): call(functools.partial(tail_kernel, scan_size, depth_size, block), (shape...  50.9 us
    pallas_call x1, Pallas kernels, on_device(): call(functools.partial(band_kernel, scan_size), shape((scan_size,) + obje...  44.5 us
    pallas_call x1, Pallas kernels, on_device(): call(functools.partial(wave_kernel, pos, rows, size, depth_size), shape((...  38.1 us
    pallas_call x1, Pallas kernels, on_device(): call(functools.partial(grad_kernel, pos, rows, size, depth_size), (shape(...  5.14 us
    pallas_call x1, Pallas kernels, on_device(): call(functools.partial(window_kernel, pos, rows, size, cols, scan_size),...  5.08 us
    pallas_call x1, Pallas kernels, on_device(): call(functools.partial(place_kernel, scan_size, pos, rows, size, cols), s...  4.87 us
    pallas_call x1, Pallas kernels, on_device(): call(functools.partial(factor_kernel, pos, rows, size), (wide, wide), [sm...  3.82 us

profile of v2, /device:TPU:0, one launch (start us, length us, event | category | flops | bytes accessed | tf_op | source)
XLA Modules:
  0.0 161.0 jit_solution(15295120363249066364)
XLA Ops:
  0.6 0.8 copy.28
  1.4 0.7 compare_select_fusion
  2.1 0.6 gather_fusion
  2.6 0.1 add_minimum_fusion
  2.7 0.7 pad_add_fusion.1.meta
  3.4 0.6 and_select_fusion.4.start
  4.0 3.8 %shard_map.132 = (f32[2,2,128,512]{3,2,1,0:T(8,128)}, f32[2,2,128,512]{3,2,1,0:T(8,128)}) custom-call(s32[2]{0:T(128)} %and_select_fusion.4.start, bf16[2,512,512]{2,1,0:T(8,128)(2,1)} %probe.1, f32[1032,128]{1,0:T(8,128)} %constant.86.clone.row_cos, f32[1032,128]{1,0:T(8,128)} %constant.87.clone.row_sin, f32[2,512]{1,0:T(2,128)} %constant.88.clone.col), custom_call_target="tpu_custom_call" | custom-call | tf_op jit(solution)/shard_map/pallas_call | solution.py:513
  7.8 44.5 %shard_map.131.band = bf16[8,2,4,128,256]{4,3,2,1,0:T(8,128)(2,1)} custom-call(bf16[2,4,128,256]{3,2,1,0:T(8,128)(2,1)} %block.1), custom_call_target="tpu_custom_call" | custom-call | tf_op jit(solution)/shard_map/pallas_call | solution.py:521
  52.3 0.0 copy-start
  52.4 5.1 %shard_map.133 = (f32[2,2,128,512]{3,2,1,0:T(8,128)}, f32[256,1024]{1,0:T(8,128)}) custom-call(s32[2,4]{1,0:T(2,128)} %pad_add_fusion.1.meta, bf16[8,2,4,128,256]{4,3,2,1,0:T(8,128)(2,1)} %shard_map.131.band, f32[2,2,128,512]{3,2,1,0:T(8,128)} %get-tuple-element.12.pc), custom_call_target="tpu_custom_call" | custom-call | tf_op jit(solution)/shard_map/pallas_call | solution.py:529
  57.4 0.0 copy-done
  57.4 1.0 copy.32.data
  58.4 38.1 %shard_map.134.back = f32[256,1024]{1,0:T(8,128)} custom-call(f32[256,1024]{1,0:T(8,128)} %get-tuple-element.13.psi, f32[512,256]{1,0:T(8,128)} %copy.32.data, bf16[4,256,1024]{2,1,0:T(8,128)(2,1)} %constant.89.clone.row_high, bf16[4,256,1024]{2,1,0:T(8,128)(2,1)} %constant.90.clone.row_low, bf16[4,1024,256]{2,1,0:T(8,128)(2,1)} %constant.91.clone.col_high, ...), custom_call_target="tpu_custom_call" | custom-call | tf_op jit(solution)/shard_map/pallas_call | solution.py:537
  96.5 0.6 convert_element_type.10.place
  97.1 5.1 %shard_map.135 = (s16[2,2,128,512]{3,2,1,0:T(8,128)(2,1)}, f32[2,16,128]{2,1,0:T(8,128)}, f32[4,2,128,512]{3,2,1,0:T(8,128)}) custom-call(s32[2]{0:T(128)} %and_select_fusion.4.start, f32[2,2]{1,0:T(2,128)} %convert_element_type.10.place, f32[256,1024]{1,0:T(8,128)} %shard_map.134.back, f32[2,2,128,512]{3,2,1,0:T(8,128)} %get-tuple-element.14.patch, ...), custom_call_target="tpu_custom_call" | custom-call | tf_op jit(solution)/shard_map/pallas_call | solution.py:545
  102.3 50.9 %shard_map.136 = (s16[8,2,2,128,512]{4,3,2,1,0:T(8,128)(2,1)}, f32[8,2,16,128]{3,2,1,0:T(8,128)}, f32[2,128,512]{2,1,0:T(8,128)}) custom-call(s16[2,2,128,512]{3,2,1,0:T(8,128)(2,1)} %get-tuple-element.16.codes, f32[2,16,128]{2,1,0:T(8,128)} %get-tuple-element.17.aux, f32[4,2,128,512]{3,2,1,0:T(8,128)} %get-tuple-element.18.probe), custom_call_target="tpu_custom_call" | custom-call | tf_op jit(solution)/shard_map/pallas_call | solution.py:557
  153.1 1.2 convert_reduce_fusion
  154.3 0.1 fusion.3
  154.4 0.1 copy.34
  154.5 0.1 copy.35
  154.6 0.7 copy.31.meta
  155.3 0.0 copy-start.1
  155.3 4.9 %shard_map.137 = f32[2,4,128,256]{3,2,1,0:T(8,128)} custom-call(s32[16,4]{1,0:T(8,128)} %copy.31.meta, s16[8,2,2,128,512]{4,3,2,1,0:T(8,128)(2,1)} %get-tuple-element.20.codes, f32[8,2,16,128]{3,2,1,0:T(8,128)} %get-tuple-element.19.aux), custom_call_target="tpu_custom_call" | custom-call | tf_op jit(solution)/shard_map/pallas_call | solution.py:574
  160.1 0.0 copy-done.1
  160.2 0.8 broadcast_multiply_fusion
  (3 shorter events, 0.0 us)
Async XLA Ops:
  52.3 5.1 %copy-start = (f32[2,128,512]{2,1,0:T(8,128)S(1)}, f32[2,128,512]{2,1,0:T(8,128)}, u32[]{:S(2)}) copy-start(f32[2,128,512]{2,1,0:T(8,128)} %param.16) | copy-start | bytes 1572868
  155.3 4.9 %copy-start.1 = (f32[2,128,512]{2,1,0:T(8,128)S(1)}, f32[2,128,512]{2,1,0:T(8,128)}, u32[]{:S(2)}) copy-start(f32[2,128,512]{2,1,0:T(8,128)} %get-tuple-element.21) | copy-start | bytes 1572868

commit v3 on v2

--- a/solution.py
+++ b/solution.py
@@ -135,26 +135,34 @@
                 for move in self.moves(block, "side"):
                     move.start()
 
+    def own_wait(self):
+        for i, (ref, out) in enumerate(self.pairs):
+            pltpu.make_async_copy(ref, out.at[self.me], self.own_sem.at[i]).wait()
+
+    def side_wait(self, t, then=None):
+        for shift in (-1, 1) if t else (0,):
+            @pl.when(self.has(shift * t))
+            def _():
+                block = self.other + 2 * shift * t
+                for move in self.moves(block, "side"):
+                    move.wait_recv()
+                if then is not None:
+                    then(self.chip + shift * t)
+
     def finish(self):
         for t in range(self.chips):
             for shift in (-1, 1) if t else (0,):
                 @pl.when(self.has(shift * t))
                 def _():
-                    block = self.other + 2 * shift * t
-                    for move in self.moves(block, "side"):
-                        move.wait_recv()
-                    mine = self.me + 2 * shift * t
-                    for move in self.moves(mine, "side"):
+                    for move in self.moves(self.me + 2 * shift * t, "side"):
                         move.wait_send()
-        for i, (ref, out) in enumerate(self.pairs):
-            pltpu.make_async_copy(ref, out.at[self.me], self.own_sem.at[i]).wait()
-        for shift, way in ((-1, "up"), (1, "down")):
-            @pl.when(self.has(-shift))
+        for shift, way in ((1, "up"), (-1, "down")):
+            @pl.when(self.has(shift))
             def _():
                 for t in range(self.chips):
-                    @pl.when(self.has(shift * t))
+                    @pl.when(self.has(-shift * t))
                     def _():
-                        for move in self.moves(self.me + 2 * shift * t, way):
+                        for move in self.moves(self.me - 2 * shift * t, way):
                             move.wait_send()
 
 
@@ -163,51 +171,29 @@
     return [dma((count, scan))] * 4 + [dma((count,))]
 
 
-def band_kernel(scan, block, band, *sems):
-    gather = Gather(scan, [(block, band)], sems)
-    barrier = pltpu.get_barrier_semaphore()
-    pl.semaphore_wait(barrier, gather.greet(barrier))
-    gather.start()
-    for t in range(1, gather.chips):
-        gather.step(t)
-    gather.finish()
-
-
-def tail_kernel(
-    scan, depth, block, codes, aux, probe, all_codes, all_aux, result,
-    land, acc, near, below, above, up_out, down_out, final, *sems
-):
-    gather = Gather(scan, [(codes, all_codes), (aux, all_aux)], sems[:5])
-    d_send, d_recv, near_sem, up_sem, down_sem, final_sem = sems[5:]
-    me = lax.axis_index("depth")
-    barrier = pltpu.get_barrier_semaphore()
+def probe_reduce(gather, me, probe, result, near, half, land, below, above, up_out, down_out, final, sems):
+    near_sem, d_send, d_recv, up_sem, down_sem, final_sem = sems
+    depth = half.shape[0]
+    core = gather.core
     partners = [lax.rem(me + i, depth) for i in range(1, depth)]
     sources = [lax.rem(me + depth - i, depth) for i in range(1, depth)]
-    for e in partners:
-        pl.semaphore_signal(barrier, inc=1, device_id={"depth": e}, device_id_type=MESH)
-    pl.semaphore_wait(barrier, gather.greet(barrier) + (depth - 1))
-    gather.start()
-    parts = [send(probe.at[e], land.at[me], d_send.at[e], d_recv.at[me], "depth", e) for e in partners]
+    cross = send(probe.at[1 - core], near, near_sem.at[0], near_sem.at[1], "scan", gather.other)
+    cross.start()
+    cross.wait_recv()
+    half[...] = probe[core] + near[...]
+    parts = [send(half.at[e], land.at[me], d_send.at[e], d_recv.at[me], "depth", e) for e in partners]
     for copy in parts:
         copy.start()
     gather.step(1)
-    total = probe[me]
+    mine = half[me]
     for e in sources:
-        send(probe.at[e], land.at[e], d_send.at[e], d_recv.at[e], "depth", e).wait_recv()
-        total = total + land[e]
-    acc[...] = total
-    core = gather.core
-    cross = send(acc.at[1 - core], near, near_sem.at[0], near_sem.at[1], "scan", gather.other)
-    cross.start()
-    for t in range(2, gather.chips - 1):
-        gather.step(t)
-    cross.wait_recv()
-    up = send(up_out, below, up_sem.at[0], up_sem.at[1], "scan", gather.me + 2)
-    down = send(down_out, above, down_sem.at[0], down_sem.at[1], "scan", gather.me - 2)
-    mine = acc[core] + near[...]
+        send(half.at[e], land.at[e], d_send.at[e], d_recv.at[e], "depth", e).wait_recv()
+        mine = mine + land[e]
     final[core] = mine
     up_out[...] = mine
     down_out[...] = mine
+    up = send(up_out, below, up_sem.at[0], up_sem.at[1], "scan", gather.me + 2)
+    down = send(down_out, above, down_sem.at[0], down_sem.at[1], "scan", gather.me - 2)
 
     @pl.when(gather.chip == 0)
     def _():
@@ -216,6 +202,9 @@
     @pl.when(gather.chip == gather.chips - 1)
     def _():
         down.start()
+
+    for t in range(2, gather.chips - 1):
+        gather.step(t)
 
     def pass_up():
         @pl.when(gather.has(-1))
@@ -257,8 +246,7 @@
         gather.step(gather.chips - 1)
     send(final.at[1 - core], final.at[1 - core], final_sem.at[0], final_sem.at[1], "scan",
          gather.other).wait_recv()
-    result[...] = final[...]
-    gather.finish()
+    result[...] = final[...] * (gather.scan * gather.pos) ** (-0.5)
     last.wait_send()
     cross.wait_send()
     for copy in parts:
@@ -273,18 +261,13 @@
         down.wait_send()
 
 
-def wave_kernel(
-    pos, rows, size, depth, psi, data, row_high, row_low, col_high, col_low, back,
+def wave_part(
+    me, pos, rows, size, depth, psi, data, row_high, row_low, col_high, col_low, back,
     out1, land1, out2, land2, far, resid, send1, recv1, send2, recv2
 ):
-    me = lax.axis_index("depth")
     block = size // depth
     partners = [lax.rem(me + i, depth) for i in range(1, depth)]
     sources = [lax.rem(me + depth - i, depth) for i in range(1, depth)]
-    barrier = pltpu.get_barrier_semaphore()
-    for e in partners:
-        pl.semaphore_signal(barrier, inc=1, device_id={"depth": e}, device_id_type=MESH)
-    pl.semaphore_wait(barrier, depth - 1)
 
     def to_rows(chunk, count, side):
         re = [chunk[p * count : (p + 1) * count, :side] for p in range(pos)]
@@ -339,42 +322,54 @@
         copy.wait_send()
 
 
-def factor_kernel(pos, rows, size, start, probe, row_cos, row_sin, col, chirp, pc, doubled):
-    doubled[:, :size] = probe[...].astype(jnp.float32)
-    doubled[:, size : 2 * size] = doubled[:, :size]
-    doubled[:, 2 * size :] = jnp.zeros_like(doubled[:, 2 * size :])
+def wrap_hot(rows, size, start, axis):
+    shape = (rows, size) if axis == 0 else (size, rows)
+    spot = lax.broadcasted_iota(jnp.int32, shape, axis) + start
+    spot = jnp.where(spot >= size, spot - size, spot)
+    return spot == lax.broadcasted_iota(jnp.int32, shape, 1 - axis)
+
+
+def as_ones(mask):
+    return jnp.where(mask, 1.0, 0.0).astype(jnp.bfloat16)
+
+
+def factor_part(pos, rows, size, start, probe, col, chirp, pc):
     cc, cs = col[0:1, :], col[1:2, :]
     for p in range(pos):
-        here = pl.ds(pl.multiple_of(start[p] // SUB * SUB, SUB), rows + SUB)
-        turn = (rows + SUB - start[p] % SUB) % (rows + SUB)
-        rc = pltpu.roll(row_cos[here, :], turn, 0)[:rows, 0:1]
-        rs = pltpu.roll(row_sin[here, :], turn, 0)[:rows, 0:1]
+        hot = wrap_hot(rows, size, start[p], 0)
+        rc = jnp.sum(jnp.where(hot, cc, 0.0), axis=1, keepdims=True)
+        rs = jnp.sum(jnp.where(hot, cs, 0.0), axis=1, keepdims=True)
+        ones = as_ones(hot)
+        pr_re, pr_im = dot(ones, probe[0]), dot(ones, probe[1])
         ch_re = rc * cc - rs * cs
         ch_im = rs * cc + rc * cs
-        pr_re = pltpu.roll(doubled[0, here, :], turn, 0)[:rows]
-        pr_im = pltpu.roll(doubled[1, here, :], turn, 0)[:rows]
         chirp[p, 0] = ch_re
         chirp[p, 1] = ch_im
         pc[p, 0] = pr_re * ch_re - pr_im * ch_im
         pc[p, 1] = pr_re * ch_im + pr_im * ch_re
 
 
-def window_kernel(pos, rows, size, cols, scan, meta, band, pc, patch, psi):
-    count = -(-(size + cols) // LANE) * LANE // cols
-    span = count * cols
-    ids = lax.broadcasted_iota(jnp.int32, (rows, size), 0)
+def window_add(pos, rows, size, cols, cycles, meta, band, patch, g):
+    row_ids = lax.broadcasted_iota(jnp.int32, (rows, cols), 0)
+    col_ids = lax.broadcasted_iota(jnp.int32, (cols, size), 0)
+    out_ids = lax.broadcasted_iota(jnp.int32, (cols, size), 1)
     for p in range(pos):
-        first, second, left, cut = meta[p, 0], meta[p, 1], meta[p, 2], meta[p, 3]
-        turn = (span - left % cols) % span
+        first, second, left, cut = meta[p]
+        cycle = jnp.where(row_ids >= cut, first, second)
+        picked = []
         for part in range(2):
-            def tile(cycle):
-                raw = [
-                    band[jnp.minimum(left // cols + i, scan - 1), part, cycle].astype(jnp.float32)
-                    for i in range(count)
-                ]
-                return pltpu.roll(jnp.concatenate(raw, 1), turn, 1)[:, :size]
-
-            patch[p, part] = jnp.where(ids >= cut, tile(first), tile(second))
+            value = band[g, part, 0].astype(jnp.float32)
+            for c in range(1, cycles):
+                value = jnp.where(cycle == c, band[g, part, c].astype(jnp.float32), value)
+            picked.append(value)
+        ones = as_ones(col_ids + (g * cols - left) == out_ids)
+        share = dot(jnp.concatenate(picked, 0).astype(jnp.bfloat16), ones)
+        patch[p, 0] += share[:rows]
+        patch[p, 1] += share[rows:]
+
+
+def wave_start(pos, rows, size, patch, pc, psi):
+    for p in range(pos):
         o_re, o_im = patch[p, 0], patch[p, 1]
         here = pl.ds(p * rows, rows)
         psi[here, :size] = o_re * pc[p, 0] - o_im * pc[p, 1]
@@ -395,11 +390,7 @@
     return jnp.sum(jnp.where(eye, row, 0.0), axis=1, keepdims=True)
 
 
-def grad_kernel(
-    pos, rows, size, depth, start, place, back, patch, pc, chirp, codes, aux, probe, doubled
-):
-    block = size // depth
-    doubled[...] = jnp.zeros_like(doubled)
+def codes_part(pos, rows, size, place, back, pc, codes, aux):
     for p in range(pos):
         b_re = back[p * rows : (p + 1) * rows, :size]
         b_im = -back[p * rows : (p + 1) * rows, size:]
@@ -418,18 +409,101 @@
         lines = 2 * (size // LANE)
         aux[p, lines:, :] = jnp.zeros((SUB, rows), jnp.float32)
         for i in range(2):
-            aux[p, lines + i : lines + i + 1, :] = jnp.full((1, rows), place[p, i], jnp.float32)
+            aux[p, lines + i : lines + i + 1, :] = jnp.full((1, rows), place[p][i].astype(jnp.float32))
+
+
+def terms_part(pos, rows, size, depth, start, back, patch, chirp, probe):
+    block = size // depth
+    ones, values = [], []
+    for p in range(pos):
+        b_re = back[p * rows : (p + 1) * rows, :size]
+        b_im = -back[p * rows : (p + 1) * rows, size:]
         g_re = b_re * chirp[p, 0] + b_im * chirp[p, 1]
         g_im = b_im * chirp[p, 0] - b_re * chirp[p, 1]
         o_re, o_im = patch[p, 0], patch[p, 1]
-        here = pl.ds(pl.multiple_of(start[p] // SUB * SUB, SUB), rows + SUB)
-        margin = jnp.zeros((SUB, size), jnp.float32)
-        for part, value in enumerate((o_re * g_re + o_im * g_im, o_re * g_im - o_im * g_re)):
-            tall = jnp.concatenate([value, margin], axis=0)
-            doubled[part, here, :] += pltpu.roll(tall, start[p] % SUB, 0)
-    for d in range(depth):
-        low, high = d * block, (d + 1) * block
-        probe[d] = doubled[:, low:high] + doubled[:, size + low : size + high]
+        values.append(jnp.concatenate([o_re * g_re + o_im * g_im, o_re * g_im - o_im * g_re], 1))
+        ones.append(as_ones(wrap_hot(rows, size, start[p], 1)))
+    high, low = halves(jnp.concatenate(values, 0))
+    hot = jnp.concatenate(ones, 1)
+    for part in range(2):
+        lanes = slice(part * size, (part + 1) * size)
+        moved = dot(hot, high[:, lanes]) + dot(hot, low[:, lanes])
+        for d in range(depth):
+            probe[part, d] = moved[d * block : (d + 1) * block]
+
+
+def main_kernel(
+    scan, depth, cycles, cols, pos, rows, size,
+    place_ref, slab, probe_field, col, intensities, row_h, row_l, col_h, col_l,
+    all_codes, all_aux, result,
+    band, row_high, row_low, col_high, col_low, chirp, pc, data, patch, psi, back,
+    out1, land1, out2, land2, far, resid, codes, aux, probe,
+    near, half, land, below, above, up_out, down_out, final, *sems
+):
+    me = lax.axis_index("depth")
+    block = size // depth
+    first_gather = Gather(scan, [(slab, band)], sems[:5])
+    gather = Gather(scan, [(codes, all_codes), (aux, all_aux)], sems[5:10])
+    gather.pos = pos
+    send1, recv1, send2, recv2, table_sem = sems[10:15]
+    barrier = pltpu.get_barrier_semaphore()
+    for i in range(1, depth):
+        pl.semaphore_signal(
+            barrier, inc=1, device_id={"depth": lax.rem(me + i, depth)}, device_id_type=MESH
+        )
+    pl.semaphore_wait(barrier, first_gather.greet(barrier) + (depth - 1))
+    first_gather.start()
+    tables = [
+        pltpu.make_async_copy(src, dst, table_sem.at[i])
+        for i, (src, dst) in enumerate(
+            ((col_h, col_high), (col_l, col_low), (row_h, row_high), (row_l, row_low))
+        )
+    ]
+    for copy in tables:
+        copy.start()
+    place, meta, start = [], [], []
+    for p in range(pos):
+        top, left = place_ref[p, 0], place_ref[p, 1]
+        first = sum(jnp.where(top >= c * size, 1, 0) for c in range(1, cycles))
+        inner = top - first * size
+        begin = me * rows - inner
+        place.append((top, left))
+        meta.append((first, jnp.minimum(first + 1, cycles - 1), left, inner - me * rows))
+        start.append(jnp.where(begin < 0, begin + size, begin))
+    factor_part(pos, rows, size, start, probe_field, col, chirp, pc)
+    data[...] = jnp.concatenate([intensities[p].T for p in range(pos)], 1)
+    for copy in tables:
+        copy.wait()
+    patch[...] = jnp.zeros_like(patch)
+
+    def add_chip(chip):
+        def one(core, carry):
+            window_add(pos, rows, size, cols, cycles, meta, band, patch, 2 * chip + core)
+            return carry
+
+        lax.fori_loop(0, 2, one, 0)
+
+    first_gather.own_wait()
+    for t in range(1, first_gather.chips):
+        first_gather.step(t)
+        first_gather.side_wait(t - 1, add_chip)
+    first_gather.side_wait(first_gather.chips - 1, add_chip)
+    first_gather.finish()
+    wave_start(pos, rows, size, patch, pc, psi)
+    wave_part(
+        me, pos, rows, size, depth, psi, data, row_high, row_low, col_high, col_low, back,
+        out1, land1, out2, land2, far, resid, send1, recv1, send2, recv2
+    )
+    codes_part(pos, rows, size, place, back, pc, codes, aux)
+    gather.start()
+    terms_part(pos, rows, size, depth, start, back, patch, chirp, probe)
+    probe_reduce(
+        gather, me, probe, result, near, half, land, below, above, up_out, down_out, final, sems[15:]
+    )
+    gather.own_wait()
+    for t in range(gather.chips):
+        gather.side_wait(t)
+    gather.finish()
 
 
 def place_kernel(groups, pos, rows, size, cols, meta, codes, aux, grad):
@@ -501,74 +575,45 @@
         cut = top % size - depth_index * rows
         return jnp.stack([first, second, left, cut], 1).astype(jnp.int32)
 
-    place = offsets[assignment]
-    top, left = place[:, 0], place[:, 1]
-    meta = describe(top, left)
-    start = (depth_index * rows - top) % size
-
-    wide = shape((pos, 2, rows, size), f32)
-    tall = 2 * size + SUB
-    row_cos = np.ascontiguousarray(np.broadcast_to(np.resize(ch_cos, tall)[:, None], (tall, LANE)))
-    row_sin = np.ascontiguousarray(np.broadcast_to(np.resize(ch_sin, tall)[:, None], (tall, LANE)))
-    chirp, pc = call(
-        functools.partial(factor_kernel, pos, rows, size),
-        (wide, wide),
-        [sm, vm, vm, vm, vm],
-        [pltpu.VMEM((2, tall, size), f32)],
-    )(start, probe_field, row_cos, row_sin, np.stack([ch_cos, ch_sin]))
-    data = intensities.transpose(2, 0, 1).reshape(size, pos * block)
-
-    band = call(
-        functools.partial(band_kernel, scan_size),
-        shape((scan_size,) + object_slice.shape, object_slice.dtype),
-        [hbm],
-        gather_sems(scan_size, 1),
-        collective=0,
-        out_specs=hbm,
-    )(object_slice)
-    patch, psi = call(
-        functools.partial(window_kernel, pos, rows, size, cols, scan_size),
-        (wide, shape((pos * rows, 2 * size), f32)),
-        [sm, vm, vm],
-    )(meta, band, pc)
+    lines = 2 * (size // LANE) + SUB
+    wide = pltpu.VMEM((pos, 2, rows, size), f32)
+    long = pltpu.VMEM((pos * rows, 2 * size), f32)
     chunk = pltpu.VMEM((depth_size, pos * rows, 2 * block), f32)
     turned = pltpu.VMEM((depth_size, 2 * rows, pos * block), f32)
     tower = pltpu.VMEM((2 * size, pos * block), f32)
-    back = call(
-        functools.partial(wave_kernel, pos, rows, size, depth_size),
-        shape((pos * rows, 2 * size), f32),
-        [vm] * 6,
-        [chunk, chunk, turned, turned, tower, tower] + [dma((depth_size,))] * 4,
-        collective=1,
-    )(psi, data, row_high, row_low, col_high, col_low)
-    lines = 2 * (size // LANE) + SUB
-    codes, aux, probe = call(
-        functools.partial(grad_kernel, pos, rows, size, depth_size),
+    slab = pltpu.VMEM((block, size), f32)
+    stack = pltpu.VMEM((depth_size, block, size), f32)
+    pair = pltpu.VMEM((2, block, size), f32)
+    by_row = pltpu.VMEM(row_high.shape, jnp.bfloat16)
+    by_col = pltpu.VMEM(col_high.shape, jnp.bfloat16)
+    all_codes, all_aux, probe_grad = call(
+        functools.partial(
+            main_kernel, scan_size, depth_size, cycles, cols, pos, rows, size
+        ),
         (
-            shape((pos, 2, rows, size), jnp.int16),
-            shape((pos, lines, rows), f32),
-            shape((depth_size, 2, block, size), f32),
-        ),
-        [sm, sm, vm, vm, vm, vm],
-        [pltpu.VMEM((2, tall, size), f32)],
-    )(start, place.astype(f32), back, patch, pc, chirp)
-    slab = pltpu.VMEM((block, size), f32)
-    pair = pltpu.VMEM((2, block, size), f32)
-    all_codes, all_aux, probe_sum = call(
-        functools.partial(tail_kernel, scan_size, depth_size, block),
-        (
-            shape((scan_size,) + codes.shape, codes.dtype),
-            shape((scan_size,) + aux.shape, aux.dtype),
+            shape((scan_size, pos, 2, rows, size), jnp.int16),
+            shape((scan_size, pos, lines, rows), f32),
             shape((2, block, size), f32),
         ),
-        [hbm, hbm, vm],
-        [pltpu.VMEM((depth_size, 2, block, size), f32), pair, slab, slab, slab, slab, slab, pair]
+        [sm, hbm, vm, vm, vm, hbm, hbm, hbm, hbm],
+        [pltpu.VMEM((scan_size,) + object_slice.shape, object_slice.dtype)]
+        + [by_row, by_row, by_col, by_col]
+        + [wide, wide]
+        + [pltpu.VMEM((size, pos * block), f32), wide, long, long]
+        + [chunk, chunk, turned, turned, tower, tower]
+        + [pltpu.VMEM((pos, 2, rows, size), jnp.int16), pltpu.VMEM((pos, lines, rows), f32)]
+        + [pltpu.VMEM((2, depth_size, block, size), f32)]
+        + [stack, stack, stack, slab, slab, slab, slab, pair]
+        + gather_sems(scan_size, 1)
         + gather_sems(scan_size, 2)
-        + [dma((depth_size,))] * 2
-        + [dma((2,))] * 4,
-        collective=2,
+        + [dma((depth_size,))] * 4
+        + [dma((4,)), dma((2,)), dma((depth_size,)), dma((depth_size,)), dma((2,)), dma((2,)), dma((2,))],
+        collective=0,
         out_specs=(hbm, hbm, vm),
-    )(codes, aux, probe)
+    )(
+        offsets[assignment], object_slice, probe_field, np.stack([ch_cos, ch_sin]),
+        intensities, row_high, row_low, col_high, col_low,
+    )
     spots = all_aux[:, :, lines - SUB : lines - SUB + 2, 0].astype(jnp.int32).reshape(-1, 2)
     meta_all = describe(spots[:, 0], scan_index * cols - spots[:, 1])
     object_grad = call(
@@ -576,7 +621,7 @@
         shape((2, cycles, rows, cols), f32),
         [sm, vm, vm],
     )(meta_all, all_codes, all_aux)
-    return object_grad, probe_sum * (pos * scan_size) ** (-0.5)
+    return object_grad, probe_grad
 
 
 def solution(mesh):

time: 163 us -> 139 us (0.85)
  Pallas kernels: 152 us -> 130 us
  other arithmetic: 4.65 us -> 1.89 us
    pallas_call x6 -> x1, Pallas kernels: 148 us -> 126 us  [on_device(): call(functools.partial(main_kernel, scan_size, depth_size, cycles, cols,...]
where the time goes in v3:
time: 139 us; the launch traced here: 136 us
  Pallas kernels  130 us (94%)
  local copies, waits for them, and re-layouts  3.58 us (3%)
  other arithmetic  1.89 us (1%)
    pallas_call x1, Pallas kernels, on_device(): call(functools.partial(main_kernel, scan_size, depth_size, cycles, cols,...  126 us
    pallas_call x1, Pallas kernels, on_device(): call(functools.partial(place_kernel, scan_size, pos, rows, size, cols), s...  4.04 us

profile of v3, /device:TPU:0, one launch (start us, length us, event | category | flops | bytes accessed | tf_op | source)
XLA Modules:
  0.0 136.3 jit_solution(18011630622198448084)
XLA Ops:
  0.6 0.7 compare_select_fusion
  1.3 0.8 copy.23
  2.1 1.1 gather_fusion
  3.2 126.2 %shard_map.113 = (s16[8,2,2,128,512]{4,3,2,1,0:T(8,128)(2,1)}, f32[8,2,16,128]{3,2,1,0:T(8,128)}, f32[2,128,512]{2,1,0:T(8,128)}) custom-call(s32[2,2]{1,0:T(2,128)} %gather_fusion, bf16[2,4,128,256]{3,2,1,0:T(8,128)(2,1)} %slab.1, bf16[2,512,512]{2,1,0:T(8,128)(2,1)} %probe_field.1, f32[2,512]{1,0:T(2,128)} %constant.56.clone.col, ...), custom_call_target="tpu_custom_call" | custom-call | tf_op jit(solution)/shard_map/pallas_call | solution.py:589
  129.3 1.2 convert_reduce_fusion
  130.5 0.1 fusion.1
  130.6 0.1 copy.28
  130.7 0.1 copy.27
  130.8 0.7 copy.25.meta
  131.5 0.0 copy-start
  131.5 4.0 %shard_map.114 = f32[2,4,128,256]{3,2,1,0:T(8,128)} custom-call(s32[16,4]{1,0:T(8,128)} %copy.25.meta, s16[8,2,2,128,512]{4,3,2,1,0:T(8,128)(2,1)} %get-tuple-element.6.codes, f32[8,2,16,128]{3,2,1,0:T(8,128)} %get-tuple-element.5.aux), custom_call_target="tpu_custom_call" | custom-call | tf_op jit(solution)/shard_map/pallas_call | solution.py:619
  135.5 0.0 copy-done
  135.5 0.8 copy.30
  (3 shorter events, 0.0 us)
Async XLA Ops:
  131.5 4.0 %copy-start = (f32[2,128,512]{2,1,0:T(8,128)S(1)}, f32[2,128,512]{2,1,0:T(8,128)}, u32[]{:S(2)}) copy-start(f32[2,128,512]{2,1,0:T(8,128)} %get-tuple-element.17) | copy-start | bytes 1572868
